TPU v7x, 512 devices: a whole 4x4x16 slice. The times are simulated.
512 devices in a mesh: aa: 8 (over z_hi, y), ba: 8 (over z_lo), col: 8 (over x, core).
Axes of the slice: x: 4, y: 4, z: 16 (z_hi: 2, z_lo: 8; z = z_hi * 8 + z_lo), core: 2. Of those that a mesh axis runs over, the one named last changes fastest.
Arguments:
- amplitudes: bfloat16 [384, 384, 384], P('aa', 'ba', 'col'), as said below
- factors: bfloat16 [4, 384, 384], replicated, may hold values from -0.15625 to 0.15625
- energies: float32 [384], replicated, may hold values from 0.3 to 1.5
Outputs:
- sigma: bfloat16 [384, 384, 384], P('aa', 'ba', 'col')
Inputs may be any that keep to these rules, and one draw needn't show every extreme that they name: amplitudes is antisymmetric: exchanging any two of its three indices changes its sign.
All inputs are finite; a program needn't handle non-finite values.
Results may differ from a plain program's by a relative error of at most 0.0065.
Values may be sent and summed in bfloat16 or wider, within the bound.
No kernel may reach another device: no remote copies, remote signals or barrier semaphores. Data moves between devices by JAX's collectives and lax.ppermute only.
A program may use at most 128 MiB of HBM per device.

v0:
```python
import jax
import jax.numpy as jnp
from jax import lax
from jax.sharding import Mesh, PartitionSpec as P

ALL = ("zh", "y", "zl", "x", "core")
PLANE = ("y", "x", "core")


def moved(array, place):
    pairs = []
    for i in range(8):
        for j in range(8):
            for k in range(8):
                a, b, c = place(i, j, k)
                pairs.append(((a * 8 + b) * 8 + c, (i * 8 + j) * 8 + k))
    return lax.ppermute(array, ALL, pairs)


def on_device(amplitudes, factors, energies):
    w = amplitudes.shape[0]
    half = lax.axis_index("zh")
    index_a = half * 4 + lax.axis_index("y")
    index_b = lax.axis_index("zl")
    index_c = lax.axis_index("x") * 2 + lax.axis_index("core")
    energy_a = lax.dynamic_slice_in_dim(energies, index_a * w, w, 0)
    energy_b = lax.dynamic_slice_in_dim(energies, index_b * w, w, 0)
    energy_c = lax.dynamic_slice_in_dim(energies, index_c * w, w, 0)

    parts = amplitudes.reshape(w, 24, 2, w).transpose(1, 0, 2, 3).reshape(24, w, 2 * w)
    parts = jnp.pad(parts, ((0, 8), (0, 0), (0, 0)))
    parts = lax.all_to_all(parts, PLANE, split_axis=0, concat_axis=0, tiled=True)
    rows = parts.reshape(4, 8, w, 2, w).transpose(3, 0, 2, 1, 4).reshape(2, 4 * w, 8 * w)
    near = lax.dynamic_slice_in_dim(rows, half * 4 * w, 4 * w, 2)
    across = lax.dynamic_slice_in_dim(rows, (1 - half) * 4 * w, 4 * w, 2)
    far = lax.ppermute(near, "zh", [(0, 1), (1, 0)])
    whole = jnp.concatenate(
        [jnp.concatenate([near, across], 2), jnp.concatenate([-across.transpose(0, 2, 1), far], 2)], 1
    )
    turned = jnp.where(half == 0, factors, jnp.roll(factors, 4 * w, 2))
    mine = lax.dynamic_slice_in_dim(turned, half * 4 * w, 4 * w, 1)
    along = jnp.einsum("pae,bef->bpaf", mine, whole, preferred_element_type=jnp.float32).astype(jnp.bfloat16)
    close = jnp.einsum("bpaf,pcf->bac", along, turned, preferred_element_type=jnp.float32).astype(jnp.bfloat16)
    close = close.reshape(2, 4, w, 8, w).transpose(1, 3, 2, 0, 4).reshape(32, w, 2 * w)
    close = lax.all_to_all(close, PLANE, split_axis=0, concat_axis=0, tiled=True)
    own = close[:24].reshape(24, w, 2, w).transpose(1, 0, 2, 3).reshape(w, w, w)
    flat = own.reshape(w, w * w)
    swap_ab = moved(flat, lambda i, j, k: (j, i, k)).reshape(w, w, w).transpose(1, 0, 2)
    swap_bc = moved(flat, lambda i, j, k: (i, k, j)).reshape(w, w, w).transpose(0, 2, 1)
    ladders = own.astype(jnp.float32) - swap_ab.astype(jnp.float32) - swap_bc.astype(jnp.float32)
    shifts = energy_a[:, None, None] + energy_b[None, :, None] + energy_c[None, None, :]
    result = 2.0 * ladders + shifts * amplitudes.astype(jnp.float32)
    return result.astype(jnp.bfloat16)


def solution(mesh):
    fine = Mesh(mesh.devices.reshape(2, 4, 8, 4, 2), ALL)
    place = P(("zh", "y"), "zl", ("x", "core"))
    return jax.shard_map(on_device, mesh=fine, in_specs=(place, P(), P()), out_specs=place, check_vma=False)
```

profile of v0, /device:TPU:144, one launch (start us, length us, event | category | flops | bytes accessed | tf_op | source)
XLA Modules:
  0.0 127.5 jit_solution(277398195950161914)
XLA Ops:
  0.0 1.4 %reshape.77 = bf16[24,48,96]{2,0,1:T(8,128)(2,1)S(1)} reshape(bf16[24,48,2,48]{3,2,0,1:T(2,128)(2,1)} %bitcast.59) | data formatting | bytes 442368 | tf_op jit(solution)/shard_map/reshape | solution.py:30
  1.4 0.8 pad.4
  2.2 7.4 %all-to-all-start = ((bf16[32,48,96]{2,1,0:T(8,128)(2,1)}), bf16[32,48,96]{2,1,0:T(8,128)(2,1)S(1)}, u32[]{:S(2)}, u32[]{:S(2)}) async-start(bf16[32,48,96]{2,1,0:T(8,128)(2,1)} %pad.4), calls=%async_computation | async-start | bytes 786432 | tf_op jit(solution)/shard_map/all_to_all | solution.py:32
  9.7 1.2 fusion.29
  10.9 6.6 %all-to-all-done = bf16[32,48,96]{2,1,0:T(8,128)(2,1)S(1)} async-done(((bf16[32,48,96]{2,1,0:T(8,128)(2,1)}), bf16[32,48,96]{2,1,0:T(8,128)(2,1)S(1)}, u32[]{:S(2)}, u32[]{:S(2)}) %all-to-all-start) | async-done | bytes 294944 | tf_op jit(solution)/shard_map/all_to_all | solution.py:32
  17.6 0.3 reshape.65
  17.9 0.3 copy.31
  18.3 1.3 reshape.66
  19.5 1.3 negate_bitcast_fusion
  20.8 10.9 %collective-permute-start = (bf16[2,192,192]{2,1,0:T(8,128)(2,1)S(1)}, bf16[2,192,192]{2,1,0:T(8,128)(2,1)S(1)}, u32[]{:S(2)}, u32[]{:S(2)}) collective-permute-start(bf16[2,192,192]{2,1,0:T(8,128)(2,1)S(1)} %get-tuple-element.11), channel_id=1, source_target_pairs={{0,256},{256,0},{1,257},{257,1},{2,258},{258,2},{3,259},{259,3},{4... | collective-permute-start | bytes 442376 | tf_op jit(solution)/shard_map/ppermute | solution.py:36
  31.7 1.6 %maximum_select_fusion = bf16[4,384,384]{2,1,0:T(8,128)(2,1)} fusion(bf16[4,384,384]{2,1,0:T(8,128)(2,1)S(1)} %copy-done, bf16[4,384,192]{2,1,0:T(8,128)(2,1)S(1)} %copy-done.1, bf16[4,384,192]{2,1,0:T(8,128)(2,1)S(1)} %get-tuple-element.7, pred[]{:T(512)S(6)} %eq.3), kind=kLoop, calls=%fused_computation.5 | loop fusion | flops 2949120 | bytes 3538945 | tf_op jit(solution)/shard_map/jit(_where)/select_n | solution.py:40
  33.4 15.3 %collective-permute-done = bf16[2,192,192]{2,1,0:T(8,128)(2,1)S(1)} collective-permute-done((bf16[2,192,192]{2,1,0:T(8,128)(2,1)S(1)}, bf16[2,192,192]{2,1,0:T(8,128)(2,1)S(1)}, u32[]{:S(2)}, u32[]{:S(2)}) %collective-permute-start) | collective-permute-done | bytes 147488 | tf_op jit(solution)/shard_map/ppermute | solution.py:36
  48.7 2.9 %fusion.3 = bf16[2,192,384]{2,1,0:T(8,128)(2,1)S(1)} fusion(bf16[4,384,384]{2,1,0:T(8,128)(2,1)} %maximum_select_fusion, bf16[2,192,192]{2,1,0:T(8,128)(2,1)S(1)} %collective-permute-done, bf16[2,192,192]{2,1,0:T(8,128)(2,1)S(1)} %copy.32, bf16[2,192,192]{2,1,0:T(8,128)(2,1)S(1)} %get-tuple-element.6, bf16[2,192,192]{2,1,0:T(8,128)(2,1)S(1)} %get-tuple-element.11, ...), kind=kOutput, calls=%fused_computation.4 | convolution fusion | flops 909066240 | bytes 2654212 | tf_op jit(solution)/shard_map/bpaf,pcf->bac/dot_general | solution.py:43
  51.6 0.7 reshape.67
  52.3 0.8 copy.48
  53.1 1.1 reshape.68
  54.2 5.7 %all-to-all-start.1 = ((bf16[32,48,96]{2,1,0:T(8,128)(2,1)}), bf16[32,48,96]{2,1,0:T(8,128)(2,1)S(1)}, u32[]{:S(2)}, u32[]{:S(2)}) async-start(bf16[32,48,96]{2,1,0:T(8,128)(2,1)} %reshape.68), calls=%async_computation.1 | async-start | bytes 786432 | tf_op jit(solution)/shard_map/all_to_all | solution.py:45
  60.0 7.8 %all-to-all-done.1 = bf16[32,48,96]{2,1,0:T(8,128)(2,1)S(1)} async-done(((bf16[32,48,96]{2,1,0:T(8,128)(2,1)}), bf16[32,48,96]{2,1,0:T(8,128)(2,1)S(1)}, u32[]{:S(2)}, u32[]{:S(2)}) %all-to-all-start.1) | async-done | bytes 294944 | tf_op jit(solution)/shard_map/all_to_all | solution.py:45
  68.1 0.4 fusion.28
  68.5 0.5 copy.36
  69.0 1.3 reshape_reshape.3
  70.2 1.9 %collective-permute-start.2 = (bf16[48,2304]{1,0:T(8,128)(2,1)}, bf16[48,2304]{1,0:T(8,128)(2,1)}, u32[]{:S(2)}, u32[]{:S(2)}) collective-permute-start(bf16[48,2304]{1,0:T(8,128)(2,1)} %reshape_reshape.3), channel_id=1, source_target_pairs={{0,0},{8,1},{16,2},{24,3},{32,4},{40,5},{48,6},{56,7},{1,8},{9,9},... | collective-permute-start | bytes 663560 | tf_op jit(solution)/shard_map/ppermute | solution.py:17
  72.1 15.0 %collective-permute-start.1 = (bf16[48,2304]{1,0:T(8,128)(2,1)}, bf16[48,2304]{1,0:T(8,128)(2,1)}, u32[]{:S(2)}, u32[]{:S(2)}) collective-permute-start(bf16[48,2304]{1,0:T(8,128)(2,1)} %reshape_reshape.3), channel_id=1, source_target_pairs={{0,0},{1,1},{2,2},{3,3},{4,4},{5,5},{6,6},{7,7},{64,8},{65,9},{66,... | collective-permute-start | bytes 663560 | tf_op jit(solution)/shard_map/ppermute | solution.py:17
  87.1 0.7 broadcast_add_fusion
  87.8 0.4 copy.35
  88.2 3.4 %collective-permute-done.2 = bf16[48,2304]{1,0:T(8,128)(2,1)} collective-permute-done((bf16[48,2304]{1,0:T(8,128)(2,1)}, bf16[48,2304]{1,0:T(8,128)(2,1)}, u32[]{:S(2)}, u32[]{:S(2)}) %collective-permute-start.2) | collective-permute-done | bytes 221216 | tf_op jit(solution)/shard_map/ppermute | solution.py:17
  91.6 1.7 %reshape.72 = f32[48,48,48]{2,1,0:T(8,128)S(1)} reshape(bf16[48,2304]{1,0:T(8,128)(2,1)} %collective-permute-done.2) | data formatting | bytes 663552 | tf_op jit(solution)/shard_map/convert_element_type | solution.py:50
  93.3 0.6 copy.37
  93.8 29.5 %collective-permute-done.1 = bf16[48,2304]{1,0:T(8,128)(2,1)} collective-permute-done((bf16[48,2304]{1,0:T(8,128)(2,1)}, bf16[48,2304]{1,0:T(8,128)(2,1)}, u32[]{:S(2)}, u32[]{:S(2)}) %collective-permute-start.1) | collective-permute-done | bytes 221216 | tf_op jit(solution)/shard_map/ppermute | solution.py:17
  123.3 1.7 %reshape.71 = f32[48,48,48]{2,1,0:T(8,128)S(1)} reshape(bf16[48,2304]{1,0:T(8,128)(2,1)} %collective-permute-done.1) | data formatting | bytes 663552 | tf_op jit(solution)/shard_map/convert_element_type | solution.py:50
  125.0 1.6 %fusion.6 = bf16[48,48,48]{2,0,1:T(8,128)(2,1)S(1)} fusion(f32[48,48,48]{1,0,2:T(8,128)S(1)} %copy.37, f32[48,48,48]{2,1,0:T(8,128)S(1)} %reshape.71, f32[48,24,2,48]{3,0,2,1:T(8,128)S(1)} %copy.35, bf16[48,48,48]{2,1,0:T(8,128)(2,1)} %param.3, f32[48]{0:T(128)S(1)} %get-tuple-element.13, f32[48,48]{0,1:T(8,128)} %broadcast_add_fusion), kind=kLoop, calls=%fused_computation.9 | loop fusion | flops 884736 | bytes 1778880 | tf_op jit(solution)/shard_map/convert_element_type | solution.py:53
  126.6 1.0 copy.39
  (11 shorter events, 0.6 us)
Async XLA Ops:
  1.4 8.3 %copy-start = (bf16[4,384,384]{2,1,0:T(8,128)(2,1)S(1)}, bf16[4,384,384]{2,1,0:T(8,128)(2,1)}, u32[]{:S(2)}) copy-start(bf16[4,384,384]{2,1,0:T(8,128)(2,1)} %param.4) | copy-start | bytes 3538948
  2.2 15.3 %all-to-all-start = ((bf16[32,48,96]{2,1,0:T(8,128)(2,1)}), bf16[32,48,96]{2,1,0:T(8,128)(2,1)S(1)}, u32[]{:S(2)}, u32[]{:S(2)}) async-start(bf16[32,48,96]{2,1,0:T(8,128)(2,1)} %pad.4), calls=%async_computation | async-start | bytes 786432 | tf_op jit(solution)/shard_map/all_to_all | solution.py:32
  18.2 13.4 %copy-start.1 = (bf16[4,384,192]{2,1,0:T(8,128)(2,1)S(1)}, bf16[4,384,192]{2,1,0:T(8,128)(2,1)}, u32[]{:S(2)}) copy-start(bf16[4,384,192]{2,1,0:T(8,128)(2,1)} %get-tuple-element.8) | copy-start | bytes 1769476
  20.8 27.9 %collective-permute-start = (bf16[2,192,192]{2,1,0:T(8,128)(2,1)S(1)}, bf16[2,192,192]{2,1,0:T(8,128)(2,1)S(1)}, u32[]{:S(2)}, u32[]{:S(2)}) collective-permute-start(bf16[2,192,192]{2,1,0:T(8,128)(2,1)S(1)} %get-tuple-element.11), channel_id=1, source_target_pairs={{0,256},{256,0},{1,257},{257,1},{2,258},{258,2},{3,259},{259,3},{4... | collective-permute-start | bytes 442376 | tf_op jit(solution)/shard_map/ppermute | solution.py:36
  53.1 6.8 %copy-start.2 = (f32[384]{0:T(512)S(1)}, f32[384]{0:T(512)}, u32[]{:S(2)}) copy-start(f32[384]{0:T(512)} %param.5) | copy-start | bytes 4612
  54.2 13.6 %all-to-all-start.1 = ((bf16[32,48,96]{2,1,0:T(8,128)(2,1)}), bf16[32,48,96]{2,1,0:T(8,128)(2,1)S(1)}, u32[]{:S(2)}, u32[]{:S(2)}) async-start(bf16[32,48,96]{2,1,0:T(8,128)(2,1)} %reshape.68), calls=%async_computation.1 | async-start | bytes 786432 | tf_op jit(solution)/shard_map/all_to_all | solution.py:45
  70.2 21.4 %collective-permute-start.2 = (bf16[48,2304]{1,0:T(8,128)(2,1)}, bf16[48,2304]{1,0:T(8,128)(2,1)}, u32[]{:S(2)}, u32[]{:S(2)}) collective-permute-start(bf16[48,2304]{1,0:T(8,128)(2,1)} %reshape_reshape.3), channel_id=1, source_target_pairs={{0,0},{8,1},{16,2},{24,3},{32,4},{40,5},{48,6},{56,7},{1,8},{9,9},... | collective-permute-start | bytes 663560 | tf_op jit(solution)/shard_map/ppermute | solution.py:17
  72.1 51.2 %collective-permute-start.1 = (bf16[48,2304]{1,0:T(8,128)(2,1)}, bf16[48,2304]{1,0:T(8,128)(2,1)}, u32[]{:S(2)}, u32[]{:S(2)}) collective-permute-start(bf16[48,2304]{1,0:T(8,128)(2,1)} %reshape_reshape.3), channel_id=1, source_target_pairs={{0,0},{1,1},{2,2},{3,3},{4,4},{5,5},{6,6},{7,7},{64,8},{65,9},{66,... | collective-permute-start | bytes 663560 | tf_op jit(solution)/shard_map/ppermute | solution.py:17
where the time goes:
time: 128 us
  waiting for transfers between devices  62.7 us (49%)
  starting transfers between devices  40.8 us (32%)
  local copies, waits for them, and re-layouts  15.4 us (12%)
  other arithmetic  5.48 us (4%)
  matrix products  2.9 us (2%)
    ppermute x2, waiting for transfers between devices, moved(): return lax.ppermute(array, ALL, pairs)  32.9 us
    ppermute x2, starting transfers between devices, moved(): return lax.ppermute(array, ALL, pairs)  16.9 us
    ppermute x1, waiting for transfers between devices, on_device(): far = lax.ppermute(near, 'zh', [(0, 1), (1, 0)])  15.3 us
    ppermute x1, starting transfers between devices, on_device(): far = lax.ppermute(near, 'zh', [(0, 1), (1, 0)])  10.9 us
    all_to_all x1, waiting for transfers between devices, on_device(): lax.all_to_all(close, PLANE, split_axis=0, concat_axis=0, tiled=True)  7.8 us
    all_to_all x1, starting transfers between devices, on_device(): lax.all_to_all(parts, PLANE, split_axis=0, concat_axis=0, tiled=True)  7.43 us
    all_to_all x1, waiting for transfers between devices, on_device(): lax.all_to_all(parts, PLANE, split_axis=0, concat_axis=0, tiled=True)  6.64 us
    all_to_all x1, starting transfers between devices, on_device(): lax.all_to_all(close, PLANE, split_axis=0, concat_axis=0, tiled=True)  5.68 us
  transfers between devices with their start and end apart: 5, of which 5 were waited for; matrix products, arithmetic and copies ran while one was open for 5% of the time, Pallas kernels for 0%

commit v1 on v0

v1 whole, which is shorter than its diff:
```python
import functools

import jax
import jax.numpy as jnp
import numpy as np
from jax import lax
from jax.experimental import pallas as pl
from jax.experimental.pallas import tpu as pltpu
from jax.sharding import Mesh, PartitionSpec as P

ALL = ("zh", "y", "zl", "x", "core")
PLANE = ("y", "x", "core")
UPPER = [(u, v) for u in range(4) for v in range(u, 4)]
MASKS = (389, 85, 114, 41, 49)


def slot(i, j, k):
    bits = k | (i & 3) << 3 | j << 5 | (i >> 2) << 8
    core, x_low, x_high, y_low, y_high = (bin(bits & mask).count("1") & 1 for mask in MASKS)
    return (y_high * 2 + y_low) * 8 + x_high * 4 + x_low * 2 + core


def holder(i, j, k):
    place = slot(i, j, k)
    return (((i >> 2) * 4 + place // 8) * 8 + j) * 8 + place % 8


def moved(array, target):
    pairs = []
    for i in range(8):
        for j in range(8):
            for k in range(8):
                a, b, c = target(i, j, k)
                pairs.append((holder(i, j, k), (a * 8 + b) * 8 + c))
    return lax.ppermute(array, ALL, pairs)


def sandwich(half_ref, slot_ref, rows_ref, far_ref, factors_ref, out_ref, matrix):
    w = rows_ref.shape[1]
    half = half_ref[0]
    first = half == 0
    own = pl.ds(pl.multiple_of(half * 4 * w, 64), 4 * w)
    other = pl.ds(pl.multiple_of((1 - half) * 4 * w, 64), 4 * w)
    mine = jnp.concatenate([factors_ref[p, own, :] for p in range(4)], axis=0)
    results = []
    for b in range(2):
        part = slice(b * w, (b + 1) * w)
        near = jnp.concatenate(
            [jnp.concatenate([rows_ref[y * 8 + k, :, part] for k in range(8)], axis=1) for y in range(4)], axis=0
        )
        across = jnp.where(first, near[:, 4 * w :], near[:, : 4 * w])
        below = -across.astype(jnp.float32).T.astype(jnp.bfloat16)
        blocks = {}
        for n, (u, v) in enumerate(UPPER):
            block = far_ref[:, (2 * n + b) * w : (2 * n + b + 1) * w]
            blocks[u, v] = block
            if u != v:
                blocks[v, u] = -block.astype(jnp.float32).T.astype(jnp.bfloat16)
        far = jnp.concatenate([jnp.concatenate([blocks[u, v] for v in range(4)], axis=1) for u in range(4)], axis=0)
        matrix[own, :] = near
        matrix[other, :] = jnp.where(
            first, jnp.concatenate([below, far], axis=1), jnp.concatenate([far, below], axis=1)
        )
        along = jnp.dot(mine, matrix[...], preferred_element_type=jnp.float32).astype(jnp.bfloat16)
        total = jnp.zeros((4 * w, 8 * w), jnp.float32)
        for p in range(4):
            total += lax.dot_general(
                along[p * 4 * w : (p + 1) * 4 * w],
                factors_ref[p],
                (((1,), (1,)), ((), ())),
                preferred_element_type=jnp.float32,
            )
        results.append(total)
    for y in range(4):
        for k in range(8):
            tile = [r[y * w : (y + 1) * w, k * w : (k + 1) * w] for r in results]
            out_ref[slot_ref[y * 8 + k]] = jnp.concatenate(tile, axis=1).astype(jnp.bfloat16)


def finish(own_ref, ab_ref, bc_ref, amps_ref, shift_a_ref, shift_bc_ref, out_ref):
    w = amps_ref.shape[0]
    shift_bc = shift_bc_ref[...]
    turned = bc_ref[...].astype(jnp.float32).T
    rest = own_ref[...].astype(jnp.float32) - ab_ref[...].astype(jnp.float32)
    for a in range(w):
        part = slice(a * w, (a + 1) * w)
        ladder = rest[:, part] - turned[part]
        shift = shift_bc + shift_a_ref[a]
        out_ref[a] = (2.0 * ladder + shift * amps_ref[a].astype(jnp.float32)).astype(jnp.bfloat16)


def on_device(amplitudes, factors, energies):
    w = amplitudes.shape[0]
    half = lax.axis_index("zh")
    index_a = half * 4 + lax.axis_index("y")
    index_b = lax.axis_index("zl")
    index_c = lax.axis_index("x") * 2 + lax.axis_index("core")
    energy_a = lax.dynamic_slice_in_dim(energies, index_a * w, w, 0)
    energy_b = lax.dynamic_slice_in_dim(energies, index_b * w, w, 0)
    energy_c = lax.dynamic_slice_in_dim(energies, index_c * w, w, 0)
    shift_bc = energy_b[:, None] + energy_c[None, :]
    places = np.array([[[slot(h * 4 + y, j, k) for y in range(4) for k in range(8)] for j in range(8)] for h in range(2)])
    places = jnp.asarray(places, jnp.int32)[half, index_b]

    parts = amplitudes.reshape(w, 24, 2, w).transpose(1, 0, 2, 3).reshape(24, w, 2 * w)
    parts = jnp.pad(parts, ((0, 8), (0, 0), (0, 0)))
    parts = lax.all_to_all(parts, PLANE, split_axis=0, concat_axis=0, tiled=True)
    near = lax.dynamic_slice_in_dim(parts.reshape(4, 8, w, 2 * w), half * 4, 4, 1)
    near = jnp.concatenate([near[u, v] for u, v in UPPER], axis=1)
    far = lax.ppermute(near, "zh", [(0, 1), (1, 0)])
    smem = pl.BlockSpec(memory_space=pltpu.SMEM)
    vmem = pl.BlockSpec(memory_space=pltpu.VMEM)
    close = pl.pallas_call(
        sandwich,
        out_shape=jax.ShapeDtypeStruct((32, w, 2 * w), jnp.bfloat16),
        in_specs=[smem, smem, vmem, vmem, vmem],
        out_specs=vmem,
        scratch_shapes=[pltpu.VMEM((8 * w, 8 * w), jnp.bfloat16)],
        compiler_params=pltpu.CompilerParams(vmem_limit_bytes=40 << 20),
        name="sandwich",
    )(half.reshape(1), places, parts, far, factors)
    close = lax.all_to_all(close, PLANE, split_axis=0, concat_axis=0, tiled=True)[:24]
    first = close.transpose(1, 0, 2).reshape(w, w * w)
    second = close.reshape(24, w, 2, w).transpose(0, 2, 1, 3).reshape(w, w * w)
    swap_ab = moved(first, lambda i, j, k: (j, i, k))
    swap_bc = moved(second, lambda i, j, k: (i, k, j))
    own = moved(second, lambda i, j, k: (i, j, k))
    return pl.pallas_call(
        finish,
        out_shape=jax.ShapeDtypeStruct(amplitudes.shape, jnp.bfloat16),
        in_specs=[vmem, vmem, vmem, vmem, smem, vmem],
        out_specs=vmem,
        compiler_params=pltpu.CompilerParams(vmem_limit_bytes=40 << 20),
        name="finish",
    )(own, swap_ab, swap_bc, amplitudes, energy_a, shift_bc)


def solution(mesh):
    fine = Mesh(mesh.devices.reshape(2, 4, 8, 4, 2), ALL)
    place = P(("zh", "y"), "zl", ("x", "core"))
    return jax.shard_map(on_device, mesh=fine, in_specs=(place, P(), P()), out_specs=place, check_vma=False)
```

time: 128 us -> 104 us (0.81)
  the two profiles are of different devices: /device:TPU:144 before, /device:TPU:129 now
where the time goes in v1:
time: 104 us
  waiting for transfers between devices  49.4 us (48%)
  starting transfers between devices  40.5 us (39%)
  Pallas kernels  8.59 us (8%)
  local copies, waits for them, and re-layouts  4.77 us (5%)
    ppermute x3, waiting for transfers between devices, moved(): return lax.ppermute(array, ALL, pairs)  21.6 us
    ppermute x3, starting transfers between devices, moved(): return lax.ppermute(array, ALL, pairs)  17.1 us
    ppermute x1, starting transfers between devices, on_device(): far = lax.ppermute(near, 'zh', [(0, 1), (1, 0)])  10.6 us
    all_to_all x1, waiting for transfers between devices, on_device(): lax.all_to_all(parts, PLANE, split_axis=0, concat_axis=0, tiled=True)  10.2 us
    all_to_all x1, waiting for transfers between devices, on_device(): lax.all_to_all(close, PLANE, split_axis=0, concat_axis=0, tiled=True)[:24]  10.1 us
    all_to_all x1, starting transfers between devices, on_device(): lax.all_to_all(parts, PLANE, split_axis=0, concat_axis=0, tiled=True)  7.76 us
    ppermute x1, waiting for transfers between devices, on_device(): far = lax.ppermute(near, 'zh', [(0, 1), (1, 0)])  7.56 us
    all_to_all x1, starting transfers between devices, on_device(): lax.all_to_all(close, PLANE, split_axis=0, concat_axis=0, tiled=True)[:24]  5.02 us
  transfers between devices with their start and end apart: 6, of which 4 were waited for; matrix products, arithmetic and copies ran while one was open for 1% of the time, Pallas kernels for 0%

profile of v1, /device:TPU:129, one launch (start us, length us, event | category | flops | bytes accessed | tf_op | source)
XLA Modules:
  0.0 103.5 jit_solution(979288828215078658)
XLA Ops:
  0.0 1.5 %copy.11 = bf16[48,24,2,48]{3,2,0,1:T(2,128)(2,1)S(1)} copy(bf16[48,24,2,48]{3,2,1,0:T(2,128)(2,1)} %bitcast.35) | data formatting | bytes 442368 | tf_op jit(solution)/shard_map/reshape | solution.py:105
  1.5 0.3 reshape.25
  1.7 0.0 copy-start.1
  1.8 0.8 pad.4
  2.6 7.8 %all-to-all-start = ((bf16[32,48,96]{2,1,0:T(8,128)(2,1)}), bf16[32,48,96]{2,1,0:T(8,128)(2,1)S(1)}, u32[]{:S(2)}, u32[]{:S(2)}) async-start(bf16[32,48,96]{2,1,0:T(8,128)(2,1)} %pad.4), calls=%async_computation | async-start | bytes 786432 | tf_op jit(solution)/shard_map/all_to_all | solution.py:107
  10.3 10.2 %all-to-all-done.rows_ref = bf16[32,48,96]{2,1,0:T(8,128)(2,1)S(1)} async-done(((bf16[32,48,96]{2,1,0:T(8,128)(2,1)}), bf16[32,48,96]{2,1,0:T(8,128)(2,1)S(1)}, u32[]{:S(2)}, u32[]{:S(2)}) %all-to-all-start) | async-done | bytes 294944 | tf_op jit(solution)/shard_map/all_to_all | solution.py:107
  20.5 0.1 concatenate.3
  20.7 10.6 %collective-permute-start = (bf16[48,960]{1,0:T(8,128)(2,1)S(1)}, bf16[48,960]{1,0:T(8,128)(2,1)S(1)}, u32[]{:S(2)}, u32[]{:S(2)}) collective-permute-start(bf16[48,960]{1,0:T(8,128)(2,1)S(1)} %concatenate.3), channel_id=1, source_target_pairs={{0,256},{256,0},{1,257},{257,1},{2,258},{258,2},{3,259},{259,3},{4... | collective-permute-start | bytes 276488 | tf_op jit(solution)/shard_map/ppermute | solution.py:110
  31.3 0.7 fusion.slot_ref
  32.0 7.6 %collective-permute-done.far_ref = bf16[48,960]{1,0:T(8,128)(2,1)S(1)} collective-permute-done((bf16[48,960]{1,0:T(8,128)(2,1)S(1)}, bf16[48,960]{1,0:T(8,128)(2,1)S(1)}, u32[]{:S(2)}, u32[]{:S(2)}) %collective-permute-start) | collective-permute-done | bytes 92192 | tf_op jit(solution)/shard_map/ppermute | solution.py:110
  39.6 0.0 copy-done.1
  39.6 3.9 %sandwich.1 = bf16[32,48,96]{2,1,0:T(8,128)(2,1)} custom-call(s32[1]{0:T(128)} %bitcast.half_ref, s32[32]{0:T(128)S(1)} %fusion.slot_ref, bf16[32,48,96]{2,1,0:T(8,128)(2,1)S(1)} %all-to-all-done.rows_ref, bf16[48,960]{1,0:T(8,128)(2,1)S(1)} %collective-permute-done.far_ref, bf16[4,384,384]{2,1,0:T(8,128)(2,1)S(1)} %copy-done.1), custom_call_target="tpu_custom_call" | custom-call | tf_op jit(solution)/shard_map/sandwich/pallas_call | solution.py:113
  43.4 5.0 %all-to-all-start.1 = ((bf16[32,48,96]{2,1,0:T(8,128)(2,1)}), bf16[32,48,96]{2,1,0:T(8,128)(2,1)S(1)}, u32[]{:S(2)}, u32[]{:S(2)}) async-start(bf16[32,48,96]{2,1,0:T(8,128)(2,1)} %sandwich.1), calls=%async_computation.1 | async-start | bytes 786432 | tf_op jit(solution)/shard_map/all_to_all | solution.py:122
  48.5 0.0 copy-done.2
  48.5 0.1 fusion.1
  48.6 10.1 %all-to-all-done.1 = bf16[32,48,96]{2,1,0:T(8,128)(2,1)S(1)} async-done(((bf16[32,48,96]{2,1,0:T(8,128)(2,1)}), bf16[32,48,96]{2,1,0:T(8,128)(2,1)S(1)}, u32[]{:S(2)}, u32[]{:S(2)}) %all-to-all-start.1) | async-done | bytes 294944 | tf_op jit(solution)/shard_map/all_to_all | solution.py:122
  58.6 0.1 slice_bitcast_fusion
  58.7 0.3 reshape.27
  59.0 0.1 copy.10
  59.1 0.0 copy-start
  59.1 0.6 reshape.28
  59.7 1.9 %collective-permute-start.3 = (bf16[48,2304]{1,0:T(8,128)(2,1)S(1)}, bf16[48,2304]{1,0:T(8,128)(2,1)S(1)}, u32[]{:S(2)}, u32[]{:S(2)}) collective-permute-start(bf16[48,2304]{1,0:T(8,128)(2,1)S(1)} %reshape.28), channel_id=1, source_target_pairs={{0,0},{195,8},{4,16},{199,24},{3,32},{192,40},{7,48},{196,56},{204... | collective-permute-start | bytes 663560 | tf_op jit(solution)/shard_map/ppermute | solution.py:35
  61.6 3.7 %collective-permute-start.1 = (bf16[48,2304]{1,0:T(8,128)(2,1)S(1)}, bf16[48,2304]{1,0:T(8,128)(2,1)S(1)}, u32[]{:S(2)}, u32[]{:S(2)}) collective-permute-start(bf16[48,2304]{1,0:T(8,128)(2,1)S(1)} %reshape.28), channel_id=1, source_target_pairs={{0,0},{195,1},{4,2},{199,3},{3,4},{192,5},{7,6},{196,7},{204,8},{1... | collective-permute-start | bytes 663560 | tf_op jit(solution)/shard_map/ppermute | solution.py:35
  65.3 0.1 copy.7
  65.4 0.2 reshape.29
  65.6 11.4 %collective-permute-start.2 = (bf16[48,2304]{1,0:T(8,128)(2,1)S(1)}, bf16[48,2304]{1,0:T(8,128)(2,1)S(1)}, u32[]{:S(2)}, u32[]{:S(2)}) collective-permute-start(bf16[48,2304]{1,0:T(8,128)(2,1)S(1)} %reshape.29), channel_id=1, source_target_pairs={{0,0},{195,1},{4,2},{199,3},{3,4},{192,5},{7,6},{196,7},{204,64},{... | collective-permute-start | bytes 663560 | tf_op jit(solution)/shard_map/ppermute | solution.py:35
  77.1 0.1 broadcast_add_fusion.shift_bc_ref
  77.1 21.6 %collective-permute-done.2.ab_ref = bf16[48,2304]{1,0:T(8,128)(2,1)S(1)} collective-permute-done((bf16[48,2304]{1,0:T(8,128)(2,1)S(1)}, bf16[48,2304]{1,0:T(8,128)(2,1)S(1)}, u32[]{:S(2)}, u32[]{:S(2)}) %collective-permute-start.2) | collective-permute-done | bytes 221216 | tf_op jit(solution)/shard_map/ppermute | solution.py:35
  98.8 0.0 collective-permute-done.3.bc_ref
  98.8 0.0 collective-permute-done.1.own_ref
  98.8 0.0 copy-done
  98.8 4.7 %finish.1 = bf16[48,48,48]{2,1,0:T(8,128)(2,1)} custom-call(bf16[48,2304]{1,0:T(8,128)(2,1)S(1)} %collective-permute-done.1.own_ref, bf16[48,2304]{1,0:T(8,128)(2,1)S(1)} %collective-permute-done.2.ab_ref, bf16[48,2304]{1,0:T(8,128)(2,1)S(1)} %collective-permute-done.3.bc_ref, bf16[48,48,48]{2,1,0:T(8,128)(2,1)S(1)} %copy-done, ...), custom_call_target="tpu_custom_call" | custom-call | tf_op jit(solution)/shard_map/finish/pallas_call | solution.py:128
  (2 shorter events, 0.0 us)
Async XLA Ops:
  1.7 37.8 %copy-start.1 = (bf16[4,384,384]{2,1,0:T(8,128)(2,1)S(1)}, bf16[4,384,384]{2,1,0:T(8,128)(2,1)}, u32[]{:S(2)}) copy-start(bf16[4,384,384]{2,1,0:T(8,128)(2,1)} %factors_ref.1) | copy-start | bytes 3538948
  2.6 17.9 %all-to-all-start = ((bf16[32,48,96]{2,1,0:T(8,128)(2,1)}), bf16[32,48,96]{2,1,0:T(8,128)(2,1)S(1)}, u32[]{:S(2)}, u32[]{:S(2)}) async-start(bf16[32,48,96]{2,1,0:T(8,128)(2,1)} %pad.4), calls=%async_computation | async-start | bytes 786432 | tf_op jit(solution)/shard_map/all_to_all | solution.py:107
  20.7 18.9 %collective-permute-start = (bf16[48,960]{1,0:T(8,128)(2,1)S(1)}, bf16[48,960]{1,0:T(8,128)(2,1)S(1)}, u32[]{:S(2)}, u32[]{:S(2)}) collective-permute-start(bf16[48,960]{1,0:T(8,128)(2,1)S(1)} %concatenate.3), channel_id=1, source_target_pairs={{0,256},{256,0},{1,257},{257,1},{2,258},{258,2},{3,259},{259,3},{4... | collective-permute-start | bytes 276488 | tf_op jit(solution)/shard_map/ppermute | solution.py:110
  39.6 8.9 %copy-start.2 = (f32[384]{0:T(512)S(1)}, f32[384]{0:T(512)}, u32[]{:S(2)}) copy-start(f32[384]{0:T(512)} %param.6) | copy-start | bytes 4612
  43.4 15.2 %all-to-all-start.1 = ((bf16[32,48,96]{2,1,0:T(8,128)(2,1)}), bf16[32,48,96]{2,1,0:T(8,128)(2,1)S(1)}, u32[]{:S(2)}, u32[]{:S(2)}) async-start(bf16[32,48,96]{2,1,0:T(8,128)(2,1)} %sandwich.1), calls=%async_computation.1 | async-start | bytes 786432 | tf_op jit(solution)/shard_map/all_to_all | solution.py:122
  59.1 39.7 %copy-start = (bf16[48,48,48]{2,1,0:T(8,128)(2,1)S(1)}, bf16[48,48,48]{2,1,0:T(8,128)(2,1)}, u32[]{:S(2)}) copy-start(bf16[48,48,48]{2,1,0:T(8,128)(2,1)} %amps_ref.1) | copy-start | bytes 663556
  59.7 39.1 %collective-permute-start.3 = (bf16[48,2304]{1,0:T(8,128)(2,1)S(1)}, bf16[48,2304]{1,0:T(8,128)(2,1)S(1)}, u32[]{:S(2)}, u32[]{:S(2)}) collective-permute-start(bf16[48,2304]{1,0:T(8,128)(2,1)S(1)} %reshape.28), channel_id=1, source_target_pairs={{0,0},{195,8},{4,16},{199,24},{3,32},{192,40},{7,48},{196,56},{204... | collective-permute-start | bytes 663560 | tf_op jit(solution)/shard_map/ppermute | solution.py:35
  61.6 37.2 %collective-permute-start.1 = (bf16[48,2304]{1,0:T(8,128)(2,1)S(1)}, bf16[48,2304]{1,0:T(8,128)(2,1)S(1)}, u32[]{:S(2)}, u32[]{:S(2)}) collective-permute-start(bf16[48,2304]{1,0:T(8,128)(2,1)S(1)} %reshape.28), channel_id=1, source_target_pairs={{0,0},{195,1},{4,2},{199,3},{3,4},{192,5},{7,6},{196,7},{204,8},{1... | collective-permute-start | bytes 663560 | tf_op jit(solution)/shard_map/ppermute | solution.py:35
  65.6 33.1 %collective-permute-start.2 = (bf16[48,2304]{1,0:T(8,128)(2,1)S(1)}, bf16[48,2304]{1,0:T(8,128)(2,1)S(1)}, u32[]{:S(2)}, u32[]{:S(2)}) collective-permute-start(bf16[48,2304]{1,0:T(8,128)(2,1)S(1)} %reshape.29), channel_id=1, source_target_pairs={{0,0},{195,1},{4,2},{199,3},{3,4},{192,5},{7,6},{196,7},{204,64},{... | collective-permute-start | bytes 663560 | tf_op jit(solution)/shard_map/ppermute | solution.py:35

commit v2 on v1

v2 whole, which is shorter than its diff:
```python
import functools

import jax
import jax.numpy as jnp
import numpy as np
from jax import lax
from jax.experimental import pallas as pl
from jax.experimental.pallas import tpu as pltpu
from jax.sharding import Mesh, PartitionSpec as P

ALL = ("zh", "y", "zl", "x", "core")
PLANE = ("y", "x", "core")
UPPER = [(u, v) for u in range(4) for v in range(u, 4)]
LAST = (((1,), (1,)), ((), ()))
MASKS = (389, 85, 114, 41, 49)


def slot(i, j, k):
    bits = k | (i & 3) << 3 | j << 5 | (i >> 2) << 8
    core, x_low, x_high, y_low, y_high = (bin(bits & mask).count("1") & 1 for mask in MASKS)
    return (y_high * 2 + y_low) * 8 + x_high * 4 + x_low * 2 + core


def holder(i, j, k):
    place = slot(i, j, k)
    return (((i >> 2) * 4 + place // 8) * 8 + j) * 8 + place % 8


def moved(array, target):
    pairs = []
    for i in range(8):
        for j in range(8):
            for k in range(8):
                a, b, c = target(i, j, k)
                pairs.append((holder(i, j, k), (a * 8 + b) * 8 + c))
    return lax.ppermute(array, ALL, pairs)


def pack(amps_ref, out_ref, rows):
    w = amps_ref.shape[0]
    rows[...] = amps_ref[...].astype(jnp.float32).reshape(w * w, w)
    for d in range(w // 2):
        pair = [rows[pl.ds(2 * d + b, w, stride=w), :] for b in range(2)]
        out_ref[d] = jnp.concatenate(pair, axis=1).astype(jnp.bfloat16)
    for d in range(w // 2, 32):
        out_ref[d] = jnp.zeros((w, 2 * w), jnp.bfloat16)


def near_part(half_ref, rows_ref, factors_ref, total_ref, other_ref, matrix):
    w = rows_ref.shape[1]
    half = half_ref[0]
    first = half == 0
    own = pl.ds(pl.multiple_of(half * 4 * w, 64), 4 * w)
    other = pl.ds(pl.multiple_of((1 - half) * 4 * w, 64), 4 * w)
    mine = jnp.concatenate([factors_ref[p, own, :] for p in range(4)], axis=0)
    for p in range(4):
        other_ref[p] = jnp.where(first, factors_ref[p, :, 4 * w :], factors_ref[p, :, : 4 * w])
    zero = jnp.zeros((4 * w, 4 * w), jnp.bfloat16)
    for b in range(2):
        part = slice(b * w, (b + 1) * w)
        near = jnp.concatenate(
            [jnp.concatenate([rows_ref[y * 8 + k, :, part] for k in range(8)], axis=1) for y in range(4)], axis=0
        )
        across = jnp.where(first, near[:, 4 * w :], near[:, : 4 * w])
        below = -across.astype(jnp.float32).T.astype(jnp.bfloat16)
        matrix[own, :] = near
        matrix[other, :] = jnp.where(
            first, jnp.concatenate([below, zero], axis=1), jnp.concatenate([zero, below], axis=1)
        )
        along = jnp.dot(mine, matrix[...], preferred_element_type=jnp.float32).astype(jnp.bfloat16)
        total = jnp.zeros((4 * w, 8 * w), jnp.float32)
        for p in range(4):
            total += lax.dot_general(
                along[p * 4 * w : (p + 1) * 4 * w], factors_ref[p], LAST, preferred_element_type=jnp.float32
            )
        total_ref[b] = total


def far_part(half_ref, slot_ref, total_ref, far_ref, other_ref, out_ref):
    w = far_ref.shape[0]
    own = pl.ds(pl.multiple_of(half_ref[0] * 4 * w, 64), 4 * w)
    mine = jnp.concatenate([other_ref[p, own, :] for p in range(4)], axis=0)
    zero = jnp.zeros((w, w), jnp.bfloat16)
    results = []
    for b in range(2):
        blocks = {at: far_ref[:, (2 * n + b) * w : (2 * n + b + 1) * w] for n, at in enumerate(UPPER)}
        upper = [[blocks[u, v] if u <= v else zero for v in range(4)] for u in range(4)]
        strict = [[blocks[u, v] if u < v else zero for v in range(4)] for u in range(4)]
        upper, strict = (
            jnp.concatenate([jnp.concatenate(line, axis=1) for line in array], axis=0) for array in (upper, strict)
        )
        along = jnp.dot(mine, upper, preferred_element_type=jnp.float32)
        along -= lax.dot_general(mine, strict, LAST, preferred_element_type=jnp.float32)
        along = along.astype(jnp.bfloat16)
        total = total_ref[b]
        for p in range(4):
            total += lax.dot_general(
                along[p * 4 * w : (p + 1) * 4 * w], other_ref[p], LAST, preferred_element_type=jnp.float32
            )
        results.append(total)
    for y in range(4):
        for k in range(8):
            tile = [r[y * w : (y + 1) * w, k * w : (k + 1) * w] for r in results]
            out_ref[slot_ref[y * 8 + k]] = jnp.concatenate(tile, axis=1).astype(jnp.bfloat16)


def begin(own_ref, bc_ref, amps_ref, shift_a_ref, shift_bc_ref, sum_ref):
    w = amps_ref.shape[0]
    shift_bc = shift_bc_ref[...]
    turned = bc_ref[...].T
    for a in range(w):
        part = slice(a * w, (a + 1) * w)
        ladder = own_ref[:, part].astype(jnp.float32) - turned[part].astype(jnp.float32)
        shift = shift_bc + shift_a_ref[a]
        sum_ref[a] = 2.0 * ladder + shift * amps_ref[a].astype(jnp.float32)


def finish(ab_ref, sum_ref, out_ref):
    w = ab_ref.shape[0]
    twice = 2.0 * ab_ref[...].astype(jnp.float32)
    for a in range(w):
        out_ref[a] = (sum_ref[a] - twice[:, a * w : (a + 1) * w]).astype(jnp.bfloat16)


def on_device(amplitudes, factors, energies):
    w = amplitudes.shape[0]
    half = lax.axis_index("zh")
    index_a = half * 4 + lax.axis_index("y")
    index_b = lax.axis_index("zl")
    index_c = lax.axis_index("x") * 2 + lax.axis_index("core")
    energy_a = lax.dynamic_slice_in_dim(energies, index_a * w, w, 0)
    energy_b = lax.dynamic_slice_in_dim(energies, index_b * w, w, 0)
    energy_c = lax.dynamic_slice_in_dim(energies, index_c * w, w, 0)
    shift_bc = energy_b[:, None] + energy_c[None, :]
    places = np.array([[[slot(h * 4 + y, j, k) for y in range(4) for k in range(8)] for j in range(8)] for h in range(2)])
    places = jnp.asarray(places, jnp.int32)[half, index_b]

    smem = pl.BlockSpec(memory_space=pltpu.SMEM)
    vmem = pl.BlockSpec(memory_space=pltpu.VMEM)
    params = pltpu.CompilerParams(vmem_limit_bytes=40 << 20)
    parts = pl.pallas_call(
        pack,
        out_shape=jax.ShapeDtypeStruct((32, w, 2 * w), jnp.bfloat16),
        in_specs=[vmem],
        out_specs=vmem,
        scratch_shapes=[pltpu.VMEM((w * w, w), jnp.float32)],
        compiler_params=params,
        name="pack",
    )(amplitudes)
    parts = lax.all_to_all(parts, PLANE, split_axis=0, concat_axis=0, tiled=True)
    near = lax.dynamic_slice_in_dim(parts.reshape(4, 8, w, 2 * w), half * 4, 4, 1)
    near = jnp.concatenate([near[u, v] for u, v in UPPER], axis=1)
    far = lax.ppermute(near, "zh", [(0, 1), (1, 0)])
    total, other = pl.pallas_call(
        near_part,
        out_shape=(
            jax.ShapeDtypeStruct((2, 4 * w, 8 * w), jnp.float32),
            jax.ShapeDtypeStruct((4, 8 * w, 4 * w), jnp.bfloat16),
        ),
        in_specs=[smem, vmem, vmem],
        out_specs=(vmem, vmem),
        scratch_shapes=[pltpu.VMEM((8 * w, 8 * w), jnp.bfloat16)],
        compiler_params=params,
        name="near_part",
    )(half.reshape(1), parts, factors)
    close = pl.pallas_call(
        far_part,
        out_shape=jax.ShapeDtypeStruct((32, w, 2 * w), jnp.bfloat16),
        in_specs=[smem, smem, vmem, vmem, vmem],
        out_specs=vmem,
        compiler_params=params,
        name="far_part",
    )(half.reshape(1), places, total, far, other)
    close = lax.all_to_all(close, PLANE, split_axis=0, concat_axis=0, tiled=True)[:24]
    first = close.transpose(1, 0, 2).reshape(w, w * w)
    second = close.reshape(24, w, 2, w).transpose(0, 2, 1, 3).reshape(w, w * w)
    swap_ab = moved(first, lambda i, j, k: (j, i, k))
    swap_bc = moved(second, lambda i, j, k: (i, k, j))
    own = moved(second, lambda i, j, k: (i, j, k))
    partial = pl.pallas_call(
        begin,
        out_shape=jax.ShapeDtypeStruct(amplitudes.shape, jnp.float32),
        in_specs=[vmem, vmem, vmem, smem, vmem],
        out_specs=vmem,
        compiler_params=params,
        name="begin",
    )(own, swap_bc, amplitudes, energy_a, shift_bc)
    return pl.pallas_call(
        finish,
        out_shape=jax.ShapeDtypeStruct(amplitudes.shape, jnp.bfloat16),
        in_specs=[vmem, vmem],
        out_specs=vmem,
        compiler_params=params,
        name="finish",
    )(swap_ab, partial)


def solution(mesh):
    fine = Mesh(mesh.devices.reshape(2, 4, 8, 4, 2), ALL)
    place = P(("zh", "y"), "zl", ("x", "core"))
    return jax.shard_map(on_device, mesh=fine, in_specs=(place, P(), P()), out_specs=place, check_vma=False)
```

time: 104 us -> 98.9 us (0.951)
  waiting for transfers between devices: 49.4 us -> 43.2 us
  Pallas kernels: 8.59 us -> 11.2 us
  local copies, waits for them, and re-layouts: 4.77 us -> 3.29 us
    pallas_call x1 -> x4, Pallas kernels: 3.86 us -> 9.97 us  [the longest x1 3.9 us: on_device(): pl.pallas_call(begin, out_shape=jax.ShapeDtypeStruct(amplitudes.shape, jn...]
    ppermute x3, waiting for transfers between devices: 21.6 us -> 17.7 us  [moved(): return lax.ppermute(array, ALL, pairs)]
    pallas_call x1, Pallas kernels: 4.73 us -> 1.23 us  [on_device(): pl.pallas_call(finish, out_shape=jax.ShapeDtypeStruct(amplitudes.shape, j...]
    ppermute x1, waiting for transfers between devices: 7.56 us -> 5.23 us  [on_device(): far = lax.ppermute(near, 'zh', [(0, 1), (1, 0)])]
    reshape x2 -> x0, local copies, waits for them, and re-layouts: 1.73 us -> none  [on_device(): amplitudes.reshape(w, 24, 2, w).transpose(1, 0, 2, 3).reshape(24, w, 2 * w)]
    unnamed x6 -> x8, local copies, waits for them, and re-layouts: 0.02 us -> 1.08 us
  transfers between devices with their start and end apart: 6 -> 6, of which waited for: 4 -> 5; matrix products, arithmetic and copies ran while one was open for 1% -> 1% of each run, Pallas kernels for 0% -> 6%
where the time goes in v2:
time: 98.9 us; the launch traced here: 98.4 us
  waiting for transfers between devices  43.2 us (44%)
  starting transfers between devices  40.5 us (41%)
  Pallas kernels  11.2 us (11%)
  local copies, waits for them, and re-layouts  3.29 us (3%)
    ppermute x3, waiting for transfers between devices, moved(): return lax.ppermute(array, ALL, pairs)  17.7 us
    ppermute x3, starting transfers between devices, moved(): return lax.ppermute(array, ALL, pairs)  17.1 us
    ppermute x1, starting transfers between devices, on_device(): far = lax.ppermute(near, 'zh', [(0, 1), (1, 0)])  10.6 us
    all_to_all x1, waiting for transfers between devices, on_device(): lax.all_to_all(parts, PLANE, split_axis=0, concat_axis=0, tiled=True)  10.2 us
    all_to_all x1, waiting for transfers between devices, on_device(): lax.all_to_all(close, PLANE, split_axis=0, concat_axis=0, tiled=True)[:24]  10.1 us
    all_to_all x1, starting transfers between devices, on_device(): lax.all_to_all(parts, PLANE, split_axis=0, concat_axis=0, tiled=True)  7.76 us
    ppermute x1, waiting for transfers between devices, on_device(): far = lax.ppermute(near, 'zh', [(0, 1), (1, 0)])  5.23 us
    all_to_all x1, starting transfers between devices, on_device(): lax.all_to_all(close, PLANE, split_axis=0, concat_axis=0, tiled=True)[:24]  5.02 us
  transfers between devices with their start and end apart: 6, of which 5 were waited for; matrix products, arithmetic and copies ran while one was open for 1% of the time, Pallas kernels for 6%

profile of v2, /device:TPU:129, one launch (start us, length us, event | category | flops | bytes accessed | tf_op | source)
XLA Modules:
  0.0 98.4 jit_solution(16807772854796450338)
XLA Ops:
  0.0 1.1 %copy-done = bf16[48,48,48]{2,1,0:T(8,128)(2,1)S(1)} copy-done((bf16[48,48,48]{2,1,0:T(8,128)(2,1)S(1)}, bf16[48,48,48]{2,1,0:T(8,128)(2,1)}, u32[]{:S(2)}) %copy-start) | copy-done | bytes 221208
  1.1 1.2 %pack.1 = bf16[32,48,96]{2,1,0:T(8,128)(2,1)} custom-call(bf16[48,48,48]{2,1,0:T(8,128)(2,1)S(1)} %copy-done), custom_call_target="tpu_custom_call" | custom-call | tf_op jit(solution)/shard_map/pack/pallas_call | solution.py:141
  2.2 7.8 %all-to-all-start = ((bf16[32,48,96]{2,1,0:T(8,128)(2,1)}), bf16[32,48,96]{2,1,0:T(8,128)(2,1)S(1)}, u32[]{:S(2)}, u32[]{:S(2)}) async-start(bf16[32,48,96]{2,1,0:T(8,128)(2,1)} %pack.1), calls=%async_computation | async-start | bytes 786432 | tf_op jit(solution)/shard_map/all_to_all | solution.py:150
  10.0 10.2 %all-to-all-done.rows_ref = bf16[32,48,96]{2,1,0:T(8,128)(2,1)S(1)} async-done(((bf16[32,48,96]{2,1,0:T(8,128)(2,1)}), bf16[32,48,96]{2,1,0:T(8,128)(2,1)S(1)}, u32[]{:S(2)}, u32[]{:S(2)}) %all-to-all-start) | async-done | bytes 294944 | tf_op jit(solution)/shard_map/all_to_all | solution.py:150
  20.2 0.1 concatenate.3
  20.3 10.6 %collective-permute-start = (bf16[48,960]{1,0:T(8,128)(2,1)S(1)}, bf16[48,960]{1,0:T(8,128)(2,1)S(1)}, u32[]{:S(2)}, u32[]{:S(2)}) collective-permute-start(bf16[48,960]{1,0:T(8,128)(2,1)S(1)} %concatenate.3), channel_id=1, source_target_pairs={{0,256},{256,0},{1,257},{257,1},{2,258},{258,2},{3,259},{259,3},{4... | collective-permute-start | bytes 276488 | tf_op jit(solution)/shard_map/ppermute | solution.py:153
  31.0 0.7 fusion.slot_ref
  31.7 0.0 copy-done.2
  31.7 2.3 %near_part.1 = (f32[2,192,384]{2,1,0:T(8,128)S(1)}, bf16[4,384,192]{2,1,0:T(8,128)(2,1)S(1)}) custom-call(s32[1]{0:T(128)} %bitcast.half_ref, bf16[32,48,96]{2,1,0:T(8,128)(2,1)S(1)} %all-to-all-done.rows_ref, bf16[4,384,384]{2,1,0:T(8,128)(2,1)S(1)} %copy-done.2), custom_call_target="tpu_custom_call" | custom-call | tf_op jit(solution)/shard_map/near_part/pallas_call | solution.py:154
  34.0 5.2 %collective-permute-done.far_ref = bf16[48,960]{1,0:T(8,128)(2,1)S(1)} collective-permute-done((bf16[48,960]{1,0:T(8,128)(2,1)S(1)}, bf16[48,960]{1,0:T(8,128)(2,1)S(1)}, u32[]{:S(2)}, u32[]{:S(2)}) %collective-permute-start) | collective-permute-done | bytes 92192 | tf_op jit(solution)/shard_map/ppermute | solution.py:153
  39.2 2.6 %far_part.1 = bf16[32,48,96]{2,1,0:T(8,128)(2,1)} custom-call(s32[1]{0:T(128)} %bitcast.half_ref, s32[32]{0:T(128)S(1)} %fusion.slot_ref, f32[2,192,384]{2,1,0:T(8,128)S(1)} %get-tuple-element.7.total_ref, bf16[48,960]{1,0:T(8,128)(2,1)S(1)} %collective-permute-done.far_ref, bf16[4,384,192]{2,1,0:T(8,128)(2,1)S(1)} %get-tuple-element.8.other_ref), custom_call_target="tpu_custom_call" | custom-call | tf_op jit(solution)/shard_map/far_part/pallas_call | solution.py:166
  41.8 5.0 %all-to-all-start.1 = ((bf16[32,48,96]{2,1,0:T(8,128)(2,1)}), bf16[32,48,96]{2,1,0:T(8,128)(2,1)S(1)}, u32[]{:S(2)}, u32[]{:S(2)}) async-start(bf16[32,48,96]{2,1,0:T(8,128)(2,1)} %far_part.1), calls=%async_computation.1 | async-start | bytes 786432 | tf_op jit(solution)/shard_map/all_to_all | solution.py:174
  46.9 0.0 copy-done.3
  46.9 0.1 fusion.2
  46.9 10.1 %all-to-all-done.1 = bf16[32,48,96]{2,1,0:T(8,128)(2,1)S(1)} async-done(((bf16[32,48,96]{2,1,0:T(8,128)(2,1)}), bf16[32,48,96]{2,1,0:T(8,128)(2,1)S(1)}, u32[]{:S(2)}, u32[]{:S(2)}) %all-to-all-start.1) | async-done | bytes 294944 | tf_op jit(solution)/shard_map/all_to_all | solution.py:174
  57.0 0.1 fusion.1
  57.1 0.3 reshape.21
  57.4 0.1 copy.8
  57.5 0.0 copy-start.1
  57.5 0.6 reshape.22
  58.1 1.9 %collective-permute-start.3 = (bf16[48,2304]{1,0:T(8,128)(2,1)S(1)}, bf16[48,2304]{1,0:T(8,128)(2,1)S(1)}, u32[]{:S(2)}, u32[]{:S(2)}) collective-permute-start(bf16[48,2304]{1,0:T(8,128)(2,1)S(1)} %reshape.22), channel_id=1, source_target_pairs={{0,0},{195,8},{4,16},{199,24},{3,32},{192,40},{7,48},{196,56},{204... | collective-permute-start | bytes 663560 | tf_op jit(solution)/shard_map/ppermute | solution.py:36
  60.0 3.7 %collective-permute-start.2 = (bf16[48,2304]{1,0:T(8,128)(2,1)S(1)}, bf16[48,2304]{1,0:T(8,128)(2,1)S(1)}, u32[]{:S(2)}, u32[]{:S(2)}) collective-permute-start(bf16[48,2304]{1,0:T(8,128)(2,1)S(1)} %reshape.22), channel_id=1, source_target_pairs={{0,0},{195,1},{4,2},{199,3},{3,4},{192,5},{7,6},{196,7},{204,8},{1... | collective-permute-start | bytes 663560 | tf_op jit(solution)/shard_map/ppermute | solution.py:36
  63.7 0.1 copy.5
  63.8 0.2 reshape.20
  64.0 11.4 %collective-permute-start.1 = (bf16[48,2304]{1,0:T(8,128)(2,1)S(1)}, bf16[48,2304]{1,0:T(8,128)(2,1)S(1)}, u32[]{:S(2)}, u32[]{:S(2)}) collective-permute-start(bf16[48,2304]{1,0:T(8,128)(2,1)S(1)} %reshape.20), channel_id=1, source_target_pairs={{0,0},{195,1},{4,2},{199,3},{3,4},{192,5},{7,6},{196,7},{204,64},{... | collective-permute-start | bytes 663560 | tf_op jit(solution)/shard_map/ppermute | solution.py:36
  75.5 0.1 broadcast_add_fusion.shift_bc_ref
  75.5 2.8 %collective-permute-done.3.bc_ref = bf16[48,2304]{1,0:T(8,128)(2,1)S(1)} collective-permute-done((bf16[48,2304]{1,0:T(8,128)(2,1)S(1)}, bf16[48,2304]{1,0:T(8,128)(2,1)S(1)}, u32[]{:S(2)}, u32[]{:S(2)}) %collective-permute-start.3) | collective-permute-done | bytes 221216 | tf_op jit(solution)/shard_map/ppermute | solution.py:36
  78.3 0.0 collective-permute-done.2.own_ref
  78.3 0.0 copy-done.1
  78.3 3.9 %begin.1.sum_ref = f32[48,48,48]{2,1,0:T(8,128)S(1)} custom-call(bf16[48,2304]{1,0:T(8,128)(2,1)S(1)} %collective-permute-done.2.own_ref, bf16[48,2304]{1,0:T(8,128)(2,1)S(1)} %collective-permute-done.3.bc_ref, bf16[48,48,48]{2,1,0:T(8,128)(2,1)S(1)} %copy-done.1, f32[48]{0:T(128)S(1)} %get-tuple-element.22.shift_a_ref, ...), custom_call_target="tpu_custom_call" | custom-call | tf_op jit(solution)/shard_map/begin/pallas_call | solution.py:180
  82.2 14.9 %collective-permute-done.1.ab_ref = bf16[48,2304]{1,0:T(8,128)(2,1)S(1)} collective-permute-done((bf16[48,2304]{1,0:T(8,128)(2,1)S(1)}, bf16[48,2304]{1,0:T(8,128)(2,1)S(1)}, u32[]{:S(2)}, u32[]{:S(2)}) %collective-permute-start.1) | collective-permute-done | bytes 221216 | tf_op jit(solution)/shard_map/ppermute | solution.py:36
  97.2 1.2 %finish.1 = bf16[48,48,48]{2,1,0:T(8,128)(2,1)} custom-call(bf16[48,2304]{1,0:T(8,128)(2,1)S(1)} %collective-permute-done.1.ab_ref, f32[48,48,48]{2,1,0:T(8,128)S(1)} %begin.1.sum_ref), custom_call_target="tpu_custom_call" | custom-call | tf_op jit(solution)/shard_map/finish/pallas_call | solution.py:188
  (4 shorter events, 0.0 us)
Async XLA Ops:
  0.0 1.1 %copy-start = (bf16[48,48,48]{2,1,0:T(8,128)(2,1)S(1)}, bf16[48,48,48]{2,1,0:T(8,128)(2,1)}, u32[]{:S(2)}) copy-start(bf16[48,48,48]{2,1,0:T(8,128)(2,1)} %amps_ref.3) | copy-start | bytes 663556
  1.1 30.6 %copy-start.2 = (bf16[4,384,384]{2,1,0:T(8,128)(2,1)S(1)}, bf16[4,384,384]{2,1,0:T(8,128)(2,1)}, u32[]{:S(2)}) copy-start(bf16[4,384,384]{2,1,0:T(8,128)(2,1)} %factors_ref.1) | copy-start | bytes 3538948
  2.2 17.9 %all-to-all-start = ((bf16[32,48,96]{2,1,0:T(8,128)(2,1)}), bf16[32,48,96]{2,1,0:T(8,128)(2,1)S(1)}, u32[]{:S(2)}, u32[]{:S(2)}) async-start(bf16[32,48,96]{2,1,0:T(8,128)(2,1)} %pack.1), calls=%async_computation | async-start | bytes 786432 | tf_op jit(solution)/shard_map/all_to_all | solution.py:150
  20.3 18.9 %collective-permute-start = (bf16[48,960]{1,0:T(8,128)(2,1)S(1)}, bf16[48,960]{1,0:T(8,128)(2,1)S(1)}, u32[]{:S(2)}, u32[]{:S(2)}) collective-permute-start(bf16[48,960]{1,0:T(8,128)(2,1)S(1)} %concatenate.3), channel_id=1, source_target_pairs={{0,256},{256,0},{1,257},{257,1},{2,258},{258,2},{3,259},{259,3},{4... | collective-permute-start | bytes 276488 | tf_op jit(solution)/shard_map/ppermute | solution.py:153
  39.2 7.6 %copy-start.3 = (f32[384]{0:T(512)S(1)}, f32[384]{0:T(512)}, u32[]{:S(2)}) copy-start(f32[384]{0:T(512)} %param.6) | copy-start | bytes 4612
  41.8 15.2 %all-to-all-start.1 = ((bf16[32,48,96]{2,1,0:T(8,128)(2,1)}), bf16[32,48,96]{2,1,0:T(8,128)(2,1)S(1)}, u32[]{:S(2)}, u32[]{:S(2)}) async-start(bf16[32,48,96]{2,1,0:T(8,128)(2,1)} %far_part.1), calls=%async_computation.1 | async-start | bytes 786432 | tf_op jit(solution)/shard_map/all_to_all | solution.py:174
  57.5 20.9 %copy-start.1 = (bf16[48,48,48]{2,1,0:T(8,128)(2,1)S(1)}, bf16[48,48,48]{2,1,0:T(8,128)(2,1)}, u32[]{:S(2)}) copy-start(bf16[48,48,48]{2,1,0:T(8,128)(2,1)} %amps_ref.3) | copy-start | bytes 663556
  58.1 20.3 %collective-permute-start.3 = (bf16[48,2304]{1,0:T(8,128)(2,1)S(1)}, bf16[48,2304]{1,0:T(8,128)(2,1)S(1)}, u32[]{:S(2)}, u32[]{:S(2)}) collective-permute-start(bf16[48,2304]{1,0:T(8,128)(2,1)S(1)} %reshape.22), channel_id=1, source_target_pairs={{0,0},{195,8},{4,16},{199,24},{3,32},{192,40},{7,48},{196,56},{204... | collective-permute-start | bytes 663560 | tf_op jit(solution)/shard_map/ppermute | solution.py:36
  60.0 18.3 %collective-permute-start.2 = (bf16[48,2304]{1,0:T(8,128)(2,1)S(1)}, bf16[48,2304]{1,0:T(8,128)(2,1)S(1)}, u32[]{:S(2)}, u32[]{:S(2)}) collective-permute-start(bf16[48,2304]{1,0:T(8,128)(2,1)S(1)} %reshape.22), channel_id=1, source_target_pairs={{0,0},{195,1},{4,2},{199,3},{3,4},{192,5},{7,6},{196,7},{204,8},{1... | collective-permute-start | bytes 663560 | tf_op jit(solution)/shard_map/ppermute | solution.py:36
  64.0 33.1 %collective-permute-start.1 = (bf16[48,2304]{1,0:T(8,128)(2,1)S(1)}, bf16[48,2304]{1,0:T(8,128)(2,1)S(1)}, u32[]{:S(2)}, u32[]{:S(2)}) collective-permute-start(bf16[48,2304]{1,0:T(8,128)(2,1)S(1)} %reshape.20), channel_id=1, source_target_pairs={{0,0},{195,1},{4,2},{199,3},{3,4},{192,5},{7,6},{196,7},{204,64},{... | collective-permute-start | bytes 663560 | tf_op jit(solution)/shard_map/ppermute | solution.py:36

commit v3 on v2

--- a/solution.py
+++ b/solution.py
@@ -172,11 +172,12 @@
         name="far_part",
     )(half.reshape(1), places, total, far, other)
     close = lax.all_to_all(close, PLANE, split_axis=0, concat_axis=0, tiled=True)[:24]
+    second = close.reshape(24, w, 2, w).transpose(0, 2, 1, 3).reshape(w, w * w)
+    swap_bc = moved(second, lambda i, j, k: (i, k, j))
     first = close.transpose(1, 0, 2).reshape(w, w * w)
-    second = close.reshape(24, w, 2, w).transpose(0, 2, 1, 3).reshape(w, w * w)
     swap_ab = moved(first, lambda i, j, k: (j, i, k))
-    swap_bc = moved(second, lambda i, j, k: (i, k, j))
-    own = moved(second, lambda i, j, k: (i, j, k))
+    third = lax.optimization_barrier(first).reshape(w, w, w).transpose(1, 0, 2).reshape(w, w * w)
+    own = moved(third, lambda i, j, k: (i, j, k))
     partial = pl.pallas_call(
         begin,
         out_shape=jax.ShapeDtypeStruct(amplitudes.shape, jnp.float32),

time: 98.9 us -> 103 us (1.041)
  the two profiles are of different devices: /device:TPU:129 before, /device:TPU:15 now
where the time goes in v3:
time: 103 us; the launch traced here: 102 us
  starting transfers between devices  55.2 us (54%)
  waiting for transfers between devices  30.6 us (30%)
  Pallas kernels  11.2 us (11%)
  local copies, waits for them, and re-layouts  4.84 us (5%)
    ppermute x3, starting transfers between devices, moved(): return lax.ppermute(array, ALL, pairs)  25.2 us
    ppermute x3, waiting for transfers between devices, moved(): return lax.ppermute(array, ALL, pairs)  14.6 us
    ppermute x1, starting transfers between devices, on_device(): far = lax.ppermute(near, 'zh', [(0, 1), (1, 0)])  13.5 us
    all_to_all x1, starting transfers between devices, on_device(): lax.all_to_all(parts, PLANE, split_axis=0, concat_axis=0, tiled=True)  9.67 us
    all_to_all x1, waiting for transfers between devices, on_device(): lax.all_to_all(parts, PLANE, split_axis=0, concat_axis=0, tiled=True)  8.02 us
    all_to_all x1, waiting for transfers between devices, on_device(): lax.all_to_all(close, PLANE, split_axis=0, concat_axis=0, tiled=True)[:24]  7.92 us
    all_to_all x1, starting transfers between devices, on_device(): lax.all_to_all(close, PLANE, split_axis=0, concat_axis=0, tiled=True)[:24]  6.76 us
    pallas_call x1, Pallas kernels, on_device(): pl.pallas_call(begin, out_shape=jax.ShapeDtypeStruct(amplitudes.shape, jn...  3.9 us
  transfers between devices with their start and end apart: 6, of which 3 were waited for; matrix products, arithmetic and copies ran while one was open for 3% of the time, Pallas kernels for 6%

profile of v3, /device:TPU:15, one launch (start us, length us, event | category | flops | bytes accessed | tf_op | source)
XLA Modules:
  0.0 102.1 jit_solution(17809068329259898819)
XLA Ops:
  0.0 1.1 %copy-done = bf16[48,48,48]{2,1,0:T(8,128)(2,1)S(1)} copy-done((bf16[48,48,48]{2,1,0:T(8,128)(2,1)S(1)}, bf16[48,48,48]{2,1,0:T(8,128)(2,1)}, u32[]{:S(2)}) %copy-start) | copy-done | bytes 221208
  1.1 1.2 %pack.1 = bf16[32,48,96]{2,1,0:T(8,128)(2,1)} custom-call(bf16[48,48,48]{2,1,0:T(8,128)(2,1)S(1)} %copy-done), custom_call_target="tpu_custom_call" | custom-call | tf_op jit(solution)/shard_map/pack/pallas_call | solution.py:141
  2.2 9.7 %all-to-all-start = ((bf16[32,48,96]{2,1,0:T(8,128)(2,1)}), bf16[32,48,96]{2,1,0:T(8,128)(2,1)S(1)}, u32[]{:S(2)}, u32[]{:S(2)}) async-start(bf16[32,48,96]{2,1,0:T(8,128)(2,1)} %pack.1), calls=%async_computation | async-start | bytes 786432 | tf_op jit(solution)/shard_map/all_to_all | solution.py:150
  11.9 8.0 %all-to-all-done.rows_ref = bf16[32,48,96]{2,1,0:T(8,128)(2,1)S(1)} async-done(((bf16[32,48,96]{2,1,0:T(8,128)(2,1)}), bf16[32,48,96]{2,1,0:T(8,128)(2,1)S(1)}, u32[]{:S(2)}, u32[]{:S(2)}) %all-to-all-start) | async-done | bytes 294944 | tf_op jit(solution)/shard_map/all_to_all | solution.py:150
  20.0 0.1 concatenate.3
  20.1 13.5 %collective-permute-start = (bf16[48,960]{1,0:T(8,128)(2,1)S(1)}, bf16[48,960]{1,0:T(8,128)(2,1)S(1)}, u32[]{:S(2)}, u32[]{:S(2)}) collective-permute-start(bf16[48,960]{1,0:T(8,128)(2,1)S(1)} %concatenate.3), channel_id=1, source_target_pairs={{0,256},{256,0},{1,257},{257,1},{2,258},{258,2},{3,259},{259,3},{4... | collective-permute-start | bytes 276488 | tf_op jit(solution)/shard_map/ppermute | solution.py:153
  33.6 0.7 fusion.slot_ref
  34.3 2.3 %near_part.1 = (f32[2,192,384]{2,1,0:T(8,128)S(1)}, bf16[4,384,192]{2,1,0:T(8,128)(2,1)S(1)}) custom-call(s32[1]{0:T(128)} %bitcast.half_ref, bf16[32,48,96]{2,1,0:T(8,128)(2,1)S(1)} %all-to-all-done.rows_ref, bf16[4,384,384]{2,1,0:T(8,128)(2,1)S(1)} %copy-done.2), custom_call_target="tpu_custom_call" | custom-call | tf_op jit(solution)/shard_map/near_part/pallas_call | solution.py:154
  36.6 0.0 collective-permute-done.far_ref
  36.7 2.6 %far_part.1 = bf16[32,48,96]{2,1,0:T(8,128)(2,1)} custom-call(s32[1]{0:T(128)} %bitcast.half_ref, s32[32]{0:T(128)S(1)} %fusion.slot_ref, f32[2,192,384]{2,1,0:T(8,128)S(1)} %get-tuple-element.7.total_ref, bf16[48,960]{1,0:T(8,128)(2,1)S(1)} %collective-permute-done.far_ref, bf16[4,384,192]{2,1,0:T(8,128)(2,1)S(1)} %get-tuple-element.8.other_ref), custom_call_target="tpu_custom_call" | custom-call | tf_op jit(solution)/shard_map/far_part/pallas_call | solution.py:166
  39.3 6.8 %all-to-all-start.1 = ((bf16[32,48,96]{2,1,0:T(8,128)(2,1)}), bf16[32,48,96]{2,1,0:T(8,128)(2,1)S(1)}, u32[]{:S(2)}, u32[]{:S(2)}) async-start(bf16[32,48,96]{2,1,0:T(8,128)(2,1)} %far_part.1), calls=%async_computation.1 | async-start | bytes 786432 | tf_op jit(solution)/shard_map/all_to_all | solution.py:174
  46.0 0.1 fusion.2
  46.1 7.9 %all-to-all-done.1 = bf16[32,48,96]{2,1,0:T(8,128)(2,1)S(1)} async-done(((bf16[32,48,96]{2,1,0:T(8,128)(2,1)}), bf16[32,48,96]{2,1,0:T(8,128)(2,1)S(1)}, u32[]{:S(2)}, u32[]{:S(2)}) %all-to-all-start.1) | async-done | bytes 294944 | tf_op jit(solution)/shard_map/all_to_all | solution.py:174
  54.0 0.1 fusion.1
  54.1 0.1 copy.5
  54.2 0.2 reshape.26
  54.4 5.1 %collective-permute-start.1 = (bf16[48,2304]{1,0:T(8,128)(2,1)S(1)}, bf16[48,2304]{1,0:T(8,128)(2,1)S(1)}, u32[]{:S(2)}, u32[]{:S(2)}) collective-permute-start(bf16[48,2304]{1,0:T(8,128)(2,1)S(1)} %reshape.26), channel_id=1, source_target_pairs={{0,0},{195,1},{4,2},{199,3},{3,4},{192,5},{7,6},{196,7},{204,64},{... | collective-permute-start | bytes 663560 | tf_op jit(solution)/shard_map/ppermute | solution.py:36
  59.5 0.3 reshape.29
  59.8 0.1 copy.9
  59.9 0.6 reshape.30
  60.5 17.8 %collective-permute-start.3 = (bf16[48,2304]{1,0:T(8,128)(2,1)S(1)}, bf16[48,2304]{1,0:T(8,128)(2,1)S(1)}, u32[]{:S(2)}, u32[]{:S(2)}) collective-permute-start(bf16[48,2304]{1,0:T(8,128)(2,1)S(1)} %reshape.30), channel_id=1, source_target_pairs={{0,0},{195,8},{4,16},{199,24},{3,32},{192,40},{7,48},{196,56},{204... | collective-permute-start | bytes 663560 | tf_op jit(solution)/shard_map/ppermute | solution.py:36
  78.3 0.8 reshape.27
  79.2 0.0 copy-start.1
  79.2 0.2 copy.6
  79.3 0.6 reshape.28
  79.9 2.3 %collective-permute-start.2 = (bf16[48,2304]{1,0:T(8,128)(2,1)S(1)}, bf16[48,2304]{1,0:T(8,128)(2,1)S(1)}, u32[]{:S(2)}, u32[]{:S(2)}) collective-permute-start(bf16[48,2304]{1,0:T(8,128)(2,1)S(1)} %reshape.28), channel_id=1, source_target_pairs={{0,0},{195,1},{4,2},{199,3},{3,4},{192,5},{7,6},{196,7},{204,8},{1... | collective-permute-start | bytes 663560 | tf_op jit(solution)/shard_map/ppermute | solution.py:36
  82.2 0.1 broadcast_add_fusion.shift_bc_ref
  82.3 14.6 %collective-permute-done.3.bc_ref = bf16[48,2304]{1,0:T(8,128)(2,1)S(1)} collective-permute-done((bf16[48,2304]{1,0:T(8,128)(2,1)S(1)}, bf16[48,2304]{1,0:T(8,128)(2,1)S(1)}, u32[]{:S(2)}, u32[]{:S(2)}) %collective-permute-start.3) | collective-permute-done | bytes 221216 | tf_op jit(solution)/shard_map/ppermute | solution.py:36
  96.9 0.0 collective-permute-done.2.own_ref
  96.9 3.9 %begin.1.sum_ref = f32[48,48,48]{2,1,0:T(8,128)S(1)} custom-call(bf16[48,2304]{1,0:T(8,128)(2,1)S(1)} %collective-permute-done.2.own_ref, bf16[48,2304]{1,0:T(8,128)(2,1)S(1)} %collective-permute-done.3.bc_ref, bf16[48,48,48]{2,1,0:T(8,128)(2,1)S(1)} %copy-done.1, f32[48]{0:T(128)S(1)} %get-tuple-element.22.shift_a_ref, ...), custom_call_target="tpu_custom_call" | custom-call | tf_op jit(solution)/shard_map/begin/pallas_call | solution.py:181
  100.8 0.0 collective-permute-done.1.ab_ref
  100.8 1.2 %finish.1 = bf16[48,48,48]{2,1,0:T(8,128)(2,1)} custom-call(bf16[48,2304]{1,0:T(8,128)(2,1)S(1)} %collective-permute-done.1.ab_ref, f32[48,48,48]{2,1,0:T(8,128)S(1)} %begin.1.sum_ref), custom_call_target="tpu_custom_call" | custom-call | tf_op jit(solution)/shard_map/finish/pallas_call | solution.py:189
  (7 shorter events, 0.0 us)
Async XLA Ops:
  0.0 1.1 %copy-start = (bf16[48,48,48]{2,1,0:T(8,128)(2,1)S(1)}, bf16[48,48,48]{2,1,0:T(8,128)(2,1)}, u32[]{:S(2)}) copy-start(bf16[48,48,48]{2,1,0:T(8,128)(2,1)} %amps_ref.3) | copy-start | bytes 663556
  1.1 33.2 %copy-start.2 = (bf16[4,384,384]{2,1,0:T(8,128)(2,1)S(1)}, bf16[4,384,384]{2,1,0:T(8,128)(2,1)}, u32[]{:S(2)}) copy-start(bf16[4,384,384]{2,1,0:T(8,128)(2,1)} %factors_ref.1) | copy-start | bytes 3538948
  2.2 17.7 %all-to-all-start = ((bf16[32,48,96]{2,1,0:T(8,128)(2,1)}), bf16[32,48,96]{2,1,0:T(8,128)(2,1)S(1)}, u32[]{:S(2)}, u32[]{:S(2)}) async-start(bf16[32,48,96]{2,1,0:T(8,128)(2,1)} %pack.1), calls=%async_computation | async-start | bytes 786432 | tf_op jit(solution)/shard_map/all_to_all | solution.py:150
  20.1 16.6 %collective-permute-start = (bf16[48,960]{1,0:T(8,128)(2,1)S(1)}, bf16[48,960]{1,0:T(8,128)(2,1)S(1)}, u32[]{:S(2)}, u32[]{:S(2)}) collective-permute-start(bf16[48,960]{1,0:T(8,128)(2,1)S(1)} %concatenate.3), channel_id=1, source_target_pairs={{0,256},{256,0},{1,257},{257,1},{2,258},{258,2},{3,259},{259,3},{4... | collective-permute-start | bytes 276488 | tf_op jit(solution)/shard_map/ppermute | solution.py:153
  36.7 9.4 %copy-start.3 = (f32[384]{0:T(512)S(1)}, f32[384]{0:T(512)}, u32[]{:S(2)}) copy-start(f32[384]{0:T(512)} %param.6) | copy-start | bytes 4612
  39.3 14.8 %all-to-all-start.1 = ((bf16[32,48,96]{2,1,0:T(8,128)(2,1)}), bf16[32,48,96]{2,1,0:T(8,128)(2,1)S(1)}, u32[]{:S(2)}, u32[]{:S(2)}) async-start(bf16[32,48,96]{2,1,0:T(8,128)(2,1)} %far_part.1), calls=%async_computation.1 | async-start | bytes 786432 | tf_op jit(solution)/shard_map/all_to_all | solution.py:174
  54.4 46.4 %collective-permute-start.1 = (bf16[48,2304]{1,0:T(8,128)(2,1)S(1)}, bf16[48,2304]{1,0:T(8,128)(2,1)S(1)}, u32[]{:S(2)}, u32[]{:S(2)}) collective-permute-start(bf16[48,2304]{1,0:T(8,128)(2,1)S(1)} %reshape.26), channel_id=1, source_target_pairs={{0,0},{195,1},{4,2},{199,3},{3,4},{192,5},{7,6},{196,7},{204,64},{... | collective-permute-start | bytes 663560 | tf_op jit(solution)/shard_map/ppermute | solution.py:36
  60.5 36.4 %collective-permute-start.3 = (bf16[48,2304]{1,0:T(8,128)(2,1)S(1)}, bf16[48,2304]{1,0:T(8,128)(2,1)S(1)}, u32[]{:S(2)}, u32[]{:S(2)}) collective-permute-start(bf16[48,2304]{1,0:T(8,128)(2,1)S(1)} %reshape.30), channel_id=1, source_target_pairs={{0,0},{195,8},{4,16},{199,24},{3,32},{192,40},{7,48},{196,56},{204... | collective-permute-start | bytes 663560 | tf_op jit(solution)/shard_map/ppermute | solution.py:36
  79.2 17.8 %copy-start.1 = (bf16[48,48,48]{2,1,0:T(8,128)(2,1)S(1)}, bf16[48,48,48]{2,1,0:T(8,128)(2,1)}, u32[]{:S(2)}) copy-start(bf16[48,48,48]{2,1,0:T(8,128)(2,1)} %amps_ref.3) | copy-start | bytes 663556
  79.9 17.0 %collective-permute-start.2 = (bf16[48,2304]{1,0:T(8,128)(2,1)S(1)}, bf16[48,2304]{1,0:T(8,128)(2,1)S(1)}, u32[]{:S(2)}, u32[]{:S(2)}) collective-permute-start(bf16[48,2304]{1,0:T(8,128)(2,1)S(1)} %reshape.28), channel_id=1, source_target_pairs={{0,0},{195,1},{4,2},{199,3},{3,4},{192,5},{7,6},{196,7},{204,8},{1... | collective-permute-start | bytes 663560 | tf_op jit(solution)/shard_map/ppermute | solution.py:36

commit v4 on v2

--- a/solution.py
+++ b/solution.py
@@ -12,17 +12,28 @@
 PLANE = ("y", "x", "core")
 UPPER = [(u, v) for u in range(4) for v in range(u, 4)]
 LAST = (((1,), (1,)), ((), ()))
-MASKS = (389, 85, 114, 41, 49)
-
-
-def slot(i, j, k):
-    bits = k | (i & 3) << 3 | j << 5 | (i >> 2) << 8
-    core, x_low, x_high, y_low, y_high = (bin(bits & mask).count("1") & 1 for mask in MASKS)
-    return (y_high * 2 + y_low) * 8 + x_high * 4 + x_low * 2 + core
+PLACES = (
+    (0, 26, 8, 4, 5, 1, 12, 30, 9, 10, 20, 2, 24, 22, 14, 6, 21, 15, 18, 28, 11, 16, 31, 23, 3, 27, 13, 17, 7, 29, 19, 25),
+    (4, 30, 2, 6, 0, 10, 31, 1, 12, 14, 15, 8, 11, 13, 16, 20, 18, 22, 28, 9, 29, 21, 24, 3, 25, 26, 19, 27, 17, 23, 5, 7),
+    (2, 24, 28, 0, 30, 6, 10, 12, 8, 31, 11, 20, 13, 4, 3, 14, 22, 16, 17, 18, 23, 19, 21, 25, 7, 1, 29, 15, 26, 27, 5, 9),
+    (6, 28, 30, 0, 12, 10, 2, 22, 20, 8, 14, 7, 11, 18, 4, 16, 26, 15, 21, 9, 13, 23, 24, 3, 5, 17, 1, 27, 31, 19, 25, 29),
+    (8, 2, 26, 3, 30, 4, 12, 0, 20, 14, 5, 9, 15, 6, 18, 16, 22, 24, 10, 25, 19, 13, 7, 21, 28, 11, 23, 17, 29, 1, 31, 27),
+    (16, 0, 4, 22, 18, 12, 24, 26, 10, 14, 15, 8, 2, 9, 11, 20, 28, 3, 1, 27, 19, 30, 23, 13, 17, 5, 6, 29, 31, 7, 25, 21),
+    (30, 12, 2, 24, 28, 14, 0, 4, 10, 16, 8, 29, 13, 6, 15, 26, 25, 11, 22, 20, 17, 21, 18, 23, 1, 27, 19, 3, 31, 7, 9, 5),
+    (8, 14, 20, 2, 24, 6, 4, 26, 16, 10, 18, 30, 5, 0, 12, 11, 17, 21, 15, 22, 9, 1, 13, 28, 3, 23, 29, 7, 25, 19, 31, 27),
+    (30, 12, 6, 2, 26, 4, 0, 18, 20, 3, 7, 8, 10, 1, 24, 13, 31, 25, 16, 27, 5, 22, 14, 21, 15, 28, 19, 17, 23, 9, 29, 11),
+    (12, 22, 28, 24, 30, 4, 8, 6, 2, 14, 10, 11, 13, 18, 7, 16, 19, 0, 20, 9, 15, 29, 25, 26, 23, 17, 21, 27, 3, 31, 5, 1),
+    (4, 12, 2, 6, 28, 18, 14, 8, 0, 3, 26, 5, 15, 7, 10, 19, 16, 22, 24, 20, 21, 27, 23, 25, 17, 30, 11, 13, 31, 29, 1, 9),
+    (24, 14, 28, 2, 8, 9, 20, 4, 15, 12, 0, 10, 21, 16, 13, 6, 22, 26, 3, 7, 11, 17, 18, 25, 5, 27, 1, 30, 23, 19, 29, 31),
+    (4, 0, 1, 12, 6, 5, 30, 2, 24, 26, 25, 22, 8, 14, 10, 20, 21, 18, 9, 16, 11, 28, 19, 15, 27, 17, 7, 29, 13, 3, 31, 23),
+    (4, 24, 18, 6, 2, 12, 0, 5, 13, 14, 10, 8, 3, 15, 9, 16, 17, 20, 22, 26, 11, 30, 1, 28, 21, 31, 25, 19, 27, 23, 29, 7),
+    (6, 26, 4, 28, 12, 7, 14, 0, 13, 8, 18, 9, 22, 10, 15, 2, 27, 29, 19, 16, 20, 24, 23, 21, 17, 30, 31, 1, 25, 3, 11, 5),
+    (30, 10, 31, 8, 16, 20, 2, 4, 14, 6, 28, 3, 9, 12, 11, 15, 22, 17, 7, 18, 0, 13, 1, 26, 27, 29, 19, 21, 5, 24, 23, 25),
+)
 
 
 def holder(i, j, k):
-    place = slot(i, j, k)
+    place = PLACES[(i >> 2) * 8 + j][(i & 3) * 8 + k]
     return (((i >> 2) * 4 + place // 8) * 8 + j) * 8 + place % 8
 
 
@@ -104,13 +115,17 @@
             out_ref[slot_ref[y * 8 + k]] = jnp.concatenate(tile, axis=1).astype(jnp.bfloat16)
 
 
-def begin(own_ref, bc_ref, amps_ref, shift_a_ref, shift_bc_ref, sum_ref):
+def begin(own_ref, bc_ref, amps_ref, shift_a_ref, shift_bc_ref, sum_ref, own_rows, bc_rows):
     w = amps_ref.shape[0]
     shift_bc = shift_bc_ref[...]
-    turned = bc_ref[...].T
+    for n in range(w):
+        part = slice(n * w, (n + 1) * w)
+        own_rows[pl.ds(n, w, stride=w), :] = own_ref[:, part].astype(jnp.float32)
+        bc_rows[pl.ds(n, w, stride=w), :] = bc_ref[:, part].astype(jnp.float32)
+    turned = bc_rows[...].T
     for a in range(w):
         part = slice(a * w, (a + 1) * w)
-        ladder = own_ref[:, part].astype(jnp.float32) - turned[part].astype(jnp.float32)
+        ladder = own_rows[part, :] - turned[:, part]
         shift = shift_bc + shift_a_ref[a]
         sum_ref[a] = 2.0 * ladder + shift * amps_ref[a].astype(jnp.float32)
 
@@ -132,8 +147,7 @@
     energy_b = lax.dynamic_slice_in_dim(energies, index_b * w, w, 0)
     energy_c = lax.dynamic_slice_in_dim(energies, index_c * w, w, 0)
     shift_bc = energy_b[:, None] + energy_c[None, :]
-    places = np.array([[[slot(h * 4 + y, j, k) for y in range(4) for k in range(8)] for j in range(8)] for h in range(2)])
-    places = jnp.asarray(places, jnp.int32)[half, index_b]
+    places = jnp.asarray(np.array(PLACES), jnp.int32)[half * 8 + index_b]
 
     smem = pl.BlockSpec(memory_space=pltpu.SMEM)
     vmem = pl.BlockSpec(memory_space=pltpu.VMEM)
@@ -173,15 +187,15 @@
     )(half.reshape(1), places, total, far, other)
     close = lax.all_to_all(close, PLANE, split_axis=0, concat_axis=0, tiled=True)[:24]
     first = close.transpose(1, 0, 2).reshape(w, w * w)
-    second = close.reshape(24, w, 2, w).transpose(0, 2, 1, 3).reshape(w, w * w)
     swap_ab = moved(first, lambda i, j, k: (j, i, k))
-    swap_bc = moved(second, lambda i, j, k: (i, k, j))
-    own = moved(second, lambda i, j, k: (i, j, k))
+    swap_bc = moved(first, lambda i, j, k: (i, k, j))
+    own = moved(first, lambda i, j, k: (i, j, k))
     partial = pl.pallas_call(
         begin,
         out_shape=jax.ShapeDtypeStruct(amplitudes.shape, jnp.float32),
         in_specs=[vmem, vmem, vmem, smem, vmem],
         out_specs=vmem,
+        scratch_shapes=[pltpu.VMEM((w * w, w), jnp.float32)] * 2,
         compiler_params=params,
         name="begin",
     )(own, swap_bc, amplitudes, energy_a, shift_bc)

time: 98.9 us -> 97 us (0.981)
  starting transfers between devices: 40.5 us -> 44.9 us
  waiting for transfers between devices: 43.2 us -> 39.4 us
  Pallas kernels: 11.2 us -> 9.46 us
    ppermute x3, starting transfers between devices: 17.1 us -> 21.3 us  [moved(): return lax.ppermute(array, ALL, pairs)]
    ppermute x3, waiting for transfers between devices: 17.7 us -> 14 us  [moved(): return lax.ppermute(array, ALL, pairs)]
    pallas_call x1, Pallas kernels: 3.9 us -> 2.16 us  [on_device(): pl.pallas_call(begin, out_shape=jax.ShapeDtypeStruct(amplitudes.shape, jn...]
  transfers between devices with their start and end apart: 6 -> 6, of which waited for: 5 -> 4; matrix products, arithmetic and copies ran while one was open for 1% -> 1% of each run, Pallas kernels for 6% -> 5%
where the time goes in v4:
time: 97 us; the launch traced here: 96.3 us
  starting transfers between devices  44.9 us (46%)
  waiting for transfers between devices  39.4 us (41%)
  Pallas kernels  9.46 us (10%)
  local copies, waits for them, and re-layouts  2.31 us (2%)
    ppermute x3, starting transfers between devices, moved(): return lax.ppermute(array, ALL, pairs)  21.3 us
    ppermute x3, waiting for transfers between devices, moved(): return lax.ppermute(array, ALL, pairs)  14 us
    ppermute x1, starting transfers between devices, on_device(): far = lax.ppermute(near, 'zh', [(0, 1), (1, 0)])  10.6 us
    all_to_all x1, waiting for transfers between devices, on_device(): lax.all_to_all(parts, PLANE, split_axis=0, concat_axis=0, tiled=True)  10.2 us
    all_to_all x1, waiting for transfers between devices, on_device(): lax.all_to_all(close, PLANE, split_axis=0, concat_axis=0, tiled=True)[:24]  10.1 us
    all_to_all x1, starting transfers between devices, on_device(): lax.all_to_all(parts, PLANE, split_axis=0, concat_axis=0, tiled=True)  7.76 us
    ppermute x1, waiting for transfers between devices, on_device(): far = lax.ppermute(near, 'zh', [(0, 1), (1, 0)])  5.23 us
    all_to_all x1, starting transfers between devices, on_device(): lax.all_to_all(close, PLANE, split_axis=0, concat_axis=0, tiled=True)[:24]  5.16 us
  transfers between devices with their start and end apart: 6, of which 4 were waited for; matrix products, arithmetic and copies ran while one was open for 1% of the time, Pallas kernels for 5%

profile of v4, /device:TPU:129, one launch (start us, length us, event | category | flops | bytes accessed | tf_op | source)
XLA Modules:
  0.0 96.3 jit_solution(2496514383281792810)
XLA Ops:
  0.0 0.0 copy-start
  0.0 1.1 %copy-done = bf16[48,48,48]{2,1,0:T(8,128)(2,1)S(1)} copy-done((bf16[48,48,48]{2,1,0:T(8,128)(2,1)S(1)}, bf16[48,48,48]{2,1,0:T(8,128)(2,1)}, u32[]{:S(2)}) %copy-start) | copy-done | bytes 221208
  1.1 0.0 copy-start.2
  1.1 1.2 %pack.1 = bf16[32,48,96]{2,1,0:T(8,128)(2,1)} custom-call(bf16[48,48,48]{2,1,0:T(8,128)(2,1)S(1)} %copy-done), custom_call_target="tpu_custom_call" | custom-call | tf_op jit(solution)/shard_map/pack/pallas_call | solution.py:155
  2.2 7.8 %all-to-all-start = ((bf16[32,48,96]{2,1,0:T(8,128)(2,1)}), bf16[32,48,96]{2,1,0:T(8,128)(2,1)S(1)}, u32[]{:S(2)}, u32[]{:S(2)}) async-start(bf16[32,48,96]{2,1,0:T(8,128)(2,1)} %pack.1), calls=%async_computation | async-start | bytes 786432 | tf_op jit(solution)/shard_map/all_to_all | solution.py:164
  10.0 10.2 %all-to-all-done.rows_ref = bf16[32,48,96]{2,1,0:T(8,128)(2,1)S(1)} async-done(((bf16[32,48,96]{2,1,0:T(8,128)(2,1)}), bf16[32,48,96]{2,1,0:T(8,128)(2,1)S(1)}, u32[]{:S(2)}, u32[]{:S(2)}) %all-to-all-start) | async-done | bytes 294944 | tf_op jit(solution)/shard_map/all_to_all | solution.py:164
  20.2 0.1 concatenate.3
  20.3 10.6 %collective-permute-start = (bf16[48,960]{1,0:T(8,128)(2,1)S(1)}, bf16[48,960]{1,0:T(8,128)(2,1)S(1)}, u32[]{:S(2)}, u32[]{:S(2)}) collective-permute-start(bf16[48,960]{1,0:T(8,128)(2,1)S(1)} %concatenate.3), channel_id=1, source_target_pairs={{0,256},{256,0},{1,257},{257,1},{2,258},{258,2},{3,259},{259,3},{4... | collective-permute-start | bytes 276488 | tf_op jit(solution)/shard_map/ppermute | solution.py:167
  31.0 0.7 fusion.slot_ref
  31.7 0.0 copy-done.2
  31.7 2.3 %near_part.1 = (f32[2,192,384]{2,1,0:T(8,128)S(1)}, bf16[4,384,192]{2,1,0:T(8,128)(2,1)S(1)}) custom-call(s32[1]{0:T(128)} %bitcast.half_ref, bf16[32,48,96]{2,1,0:T(8,128)(2,1)S(1)} %all-to-all-done.rows_ref, bf16[4,384,384]{2,1,0:T(8,128)(2,1)S(1)} %copy-done.2), custom_call_target="tpu_custom_call" | custom-call | tf_op jit(solution)/shard_map/near_part/pallas_call | solution.py:168
  34.0 5.2 %collective-permute-done.far_ref = bf16[48,960]{1,0:T(8,128)(2,1)S(1)} collective-permute-done((bf16[48,960]{1,0:T(8,128)(2,1)S(1)}, bf16[48,960]{1,0:T(8,128)(2,1)S(1)}, u32[]{:S(2)}, u32[]{:S(2)}) %collective-permute-start) | collective-permute-done | bytes 92192 | tf_op jit(solution)/shard_map/ppermute | solution.py:167
  39.2 0.0 copy-start.3
  39.2 2.6 %far_part.1 = bf16[32,48,96]{2,1,0:T(8,128)(2,1)} custom-call(s32[1]{0:T(128)} %bitcast.half_ref, s32[32]{0:T(128)S(1)} %fusion.slot_ref, f32[2,192,384]{2,1,0:T(8,128)S(1)} %get-tuple-element.7.total_ref, bf16[48,960]{1,0:T(8,128)(2,1)S(1)} %collective-permute-done.far_ref, bf16[4,384,192]{2,1,0:T(8,128)(2,1)S(1)} %get-tuple-element.8.other_ref), custom_call_target="tpu_custom_call" | custom-call | tf_op jit(solution)/shard_map/far_part/pallas_call | solution.py:180
  41.8 0.0 copy-start.1
  41.8 5.2 %all-to-all-start.1 = ((bf16[32,48,96]{2,1,0:T(8,128)(2,1)}), bf16[32,48,96]{2,1,0:T(8,128)(2,1)S(1)}, u32[]{:S(2)}, u32[]{:S(2)}) async-start(bf16[32,48,96]{2,1,0:T(8,128)(2,1)} %far_part.1), calls=%async_computation.1 | async-start | bytes 786432 | tf_op jit(solution)/shard_map/all_to_all | solution.py:188
  47.0 0.0 copy-done.3
  47.0 0.1 fusion.1
  47.1 10.1 %all-to-all-done.1 = bf16[32,48,96]{2,1,0:T(8,128)(2,1)S(1)} async-done(((bf16[32,48,96]{2,1,0:T(8,128)(2,1)}), bf16[32,48,96]{2,1,0:T(8,128)(2,1)S(1)}, u32[]{:S(2)}, u32[]{:S(2)}) %all-to-all-start.1) | async-done | bytes 294944 | tf_op jit(solution)/shard_map/all_to_all | solution.py:188
  57.2 0.1 copy.5
  57.3 0.2 reshape.14
  57.5 1.9 %collective-permute-start.3 = (bf16[48,2304]{1,0:T(8,128)(2,1)S(1)}, bf16[48,2304]{1,0:T(8,128)(2,1)S(1)}, u32[]{:S(2)}, u32[]{:S(2)}) collective-permute-start(bf16[48,2304]{1,0:T(8,128)(2,1)S(1)} %reshape.14), channel_id=1, source_target_pairs={{0,0},{194,8},{64,16},{4,24},{5,32},{1,40},{68,48},{198,56},{12,1}... | collective-permute-start | bytes 663560 | tf_op jit(solution)/shard_map/ppermute | solution.py:47
  59.4 3.5 %collective-permute-start.2 = (bf16[48,2304]{1,0:T(8,128)(2,1)S(1)}, bf16[48,2304]{1,0:T(8,128)(2,1)S(1)}, u32[]{:S(2)}, u32[]{:S(2)}) collective-permute-start(bf16[48,2304]{1,0:T(8,128)(2,1)S(1)} %reshape.14), channel_id=1, source_target_pairs={{0,0},{194,1},{64,2},{4,3},{5,4},{1,5},{68,6},{198,7},{12,8},{206,... | collective-permute-start | bytes 663560 | tf_op jit(solution)/shard_map/ppermute | solution.py:47
  62.9 15.9 %collective-permute-start.1 = (bf16[48,2304]{1,0:T(8,128)(2,1)S(1)}, bf16[48,2304]{1,0:T(8,128)(2,1)S(1)}, u32[]{:S(2)}, u32[]{:S(2)}) collective-permute-start(bf16[48,2304]{1,0:T(8,128)(2,1)S(1)} %reshape.14), channel_id=1, source_target_pairs={{0,0},{194,1},{64,2},{4,3},{5,4},{1,5},{68,6},{198,7},{12,64},{206... | collective-permute-start | bytes 663560 | tf_op jit(solution)/shard_map/ppermute | solution.py:47
  78.8 0.1 broadcast_add_fusion.shift_bc_ref
  78.9 0.0 collective-permute-done.3.bc_ref
  78.9 0.0 collective-permute-done.2.own_ref
  78.9 0.0 copy-done.1
  78.9 2.2 %begin.1.sum_ref = f32[48,48,48]{2,1,0:T(8,128)S(1)} custom-call(bf16[48,2304]{1,0:T(8,128)(2,1)S(1)} %collective-permute-done.2.own_ref, bf16[48,2304]{1,0:T(8,128)(2,1)S(1)} %collective-permute-done.3.bc_ref, bf16[48,48,48]{2,1,0:T(8,128)(2,1)S(1)} %copy-done.1, f32[48]{0:T(128)S(1)} %get-tuple-element.20.shift_a_ref, ...), custom_call_target="tpu_custom_call" | custom-call | tf_op jit(solution)/shard_map/begin/pallas_call | solution.py:193
  81.1 14.0 %collective-permute-done.1.ab_ref = bf16[48,2304]{1,0:T(8,128)(2,1)S(1)} collective-permute-done((bf16[48,2304]{1,0:T(8,128)(2,1)S(1)}, bf16[48,2304]{1,0:T(8,128)(2,1)S(1)}, u32[]{:S(2)}, u32[]{:S(2)}) %collective-permute-start.1) | collective-permute-done | bytes 221216 | tf_op jit(solution)/shard_map/ppermute | solution.py:47
  95.0 1.2 %finish.1 = bf16[48,48,48]{2,1,0:T(8,128)(2,1)} custom-call(bf16[48,2304]{1,0:T(8,128)(2,1)S(1)} %collective-permute-done.1.ab_ref, f32[48,48,48]{2,1,0:T(8,128)S(1)} %begin.1.sum_ref), custom_call_target="tpu_custom_call" | custom-call | tf_op jit(solution)/shard_map/finish/pallas_call | solution.py:202
  (2 shorter events, 0.0 us)
Async XLA Ops:
  0.0 1.1 %copy-start = (bf16[48,48,48]{2,1,0:T(8,128)(2,1)S(1)}, bf16[48,48,48]{2,1,0:T(8,128)(2,1)}, u32[]{:S(2)}) copy-start(bf16[48,48,48]{2,1,0:T(8,128)(2,1)} %amps_ref.3) | copy-start | bytes 663556
  1.1 30.6 %copy-start.2 = (bf16[4,384,384]{2,1,0:T(8,128)(2,1)S(1)}, bf16[4,384,384]{2,1,0:T(8,128)(2,1)}, u32[]{:S(2)}) copy-start(bf16[4,384,384]{2,1,0:T(8,128)(2,1)} %factors_ref.1) | copy-start | bytes 3538948
  2.2 17.9 %all-to-all-start = ((bf16[32,48,96]{2,1,0:T(8,128)(2,1)}), bf16[32,48,96]{2,1,0:T(8,128)(2,1)S(1)}, u32[]{:S(2)}, u32[]{:S(2)}) async-start(bf16[32,48,96]{2,1,0:T(8,128)(2,1)} %pack.1), calls=%async_computation | async-start | bytes 786432 | tf_op jit(solution)/shard_map/all_to_all | solution.py:164
  20.3 18.9 %collective-permute-start = (bf16[48,960]{1,0:T(8,128)(2,1)S(1)}, bf16[48,960]{1,0:T(8,128)(2,1)S(1)}, u32[]{:S(2)}, u32[]{:S(2)}) collective-permute-start(bf16[48,960]{1,0:T(8,128)(2,1)S(1)} %concatenate.3), channel_id=1, source_target_pairs={{0,256},{256,0},{1,257},{257,1},{2,258},{258,2},{3,259},{259,3},{4... | collective-permute-start | bytes 276488 | tf_op jit(solution)/shard_map/ppermute | solution.py:167
  39.2 7.8 %copy-start.3 = (f32[384]{0:T(512)S(1)}, f32[384]{0:T(512)}, u32[]{:S(2)}) copy-start(f32[384]{0:T(512)} %param.6) | copy-start | bytes 4612
  41.8 37.1 %copy-start.1 = (bf16[48,48,48]{2,1,0:T(8,128)(2,1)S(1)}, bf16[48,48,48]{2,1,0:T(8,128)(2,1)}, u32[]{:S(2)}) copy-start(bf16[48,48,48]{2,1,0:T(8,128)(2,1)} %amps_ref.3) | copy-start | bytes 663556
  41.8 15.3 %all-to-all-start.1 = ((bf16[32,48,96]{2,1,0:T(8,128)(2,1)}), bf16[32,48,96]{2,1,0:T(8,128)(2,1)S(1)}, u32[]{:S(2)}, u32[]{:S(2)}) async-start(bf16[32,48,96]{2,1,0:T(8,128)(2,1)} %far_part.1), calls=%async_computation.1 | async-start | bytes 786432 | tf_op jit(solution)/shard_map/all_to_all | solution.py:188
  57.5 21.4 %collective-permute-start.3 = (bf16[48,2304]{1,0:T(8,128)(2,1)S(1)}, bf16[48,2304]{1,0:T(8,128)(2,1)S(1)}, u32[]{:S(2)}, u32[]{:S(2)}) collective-permute-start(bf16[48,2304]{1,0:T(8,128)(2,1)S(1)} %reshape.14), channel_id=1, source_target_pairs={{0,0},{194,8},{64,16},{4,24},{5,32},{1,40},{68,48},{198,56},{12,1}... | collective-permute-start | bytes 663560 | tf_op jit(solution)/shard_map/ppermute | solution.py:47
  59.4 19.5 %collective-permute-start.2 = (bf16[48,2304]{1,0:T(8,128)(2,1)S(1)}, bf16[48,2304]{1,0:T(8,128)(2,1)S(1)}, u32[]{:S(2)}, u32[]{:S(2)}) collective-permute-start(bf16[48,2304]{1,0:T(8,128)(2,1)S(1)} %reshape.14), channel_id=1, source_target_pairs={{0,0},{194,1},{64,2},{4,3},{5,4},{1,5},{68,6},{198,7},{12,8},{206,... | collective-permute-start | bytes 663560 | tf_op jit(solution)/shard_map/ppermute | solution.py:47
  62.9 32.2 %collective-permute-start.1 = (bf16[48,2304]{1,0:T(8,128)(2,1)S(1)}, bf16[48,2304]{1,0:T(8,128)(2,1)S(1)}, u32[]{:S(2)}, u32[]{:S(2)}) collective-permute-start(bf16[48,2304]{1,0:T(8,128)(2,1)S(1)} %reshape.14), channel_id=1, source_target_pairs={{0,0},{194,1},{64,2},{4,3},{5,4},{1,5},{68,6},{198,7},{12,64},{206... | collective-permute-start | bytes 663560 | tf_op jit(solution)/shard_map/ppermute | solution.py:47

commit v5 on v4

--- a/solution.py
+++ b/solution.py
@@ -115,26 +115,25 @@
             out_ref[slot_ref[y * 8 + k]] = jnp.concatenate(tile, axis=1).astype(jnp.bfloat16)
 
 
-def begin(own_ref, bc_ref, amps_ref, shift_a_ref, shift_bc_ref, sum_ref, own_rows, bc_rows):
+def begin(bc_ref, amps_ref, shift_a_ref, shift_bc_ref, sum_ref, rows):
     w = amps_ref.shape[0]
     shift_bc = shift_bc_ref[...]
     for n in range(w):
-        part = slice(n * w, (n + 1) * w)
-        own_rows[pl.ds(n, w, stride=w), :] = own_ref[:, part].astype(jnp.float32)
-        bc_rows[pl.ds(n, w, stride=w), :] = bc_ref[:, part].astype(jnp.float32)
-    turned = bc_rows[...].T
+        rows[pl.ds(n, w, stride=w), :] = bc_ref[:, n * w : (n + 1) * w].astype(jnp.float32)
+    turned = rows[...].T
+    for a in range(w):
+        shift = shift_bc + shift_a_ref[a]
+        sum_ref[a] = shift * amps_ref[a].astype(jnp.float32) - 2.0 * turned[:, a * w : (a + 1) * w]
+
+
+def finish(own_ref, ab_ref, sum_ref, out_ref, rows):
+    w = ab_ref.shape[0]
+    for n in range(w):
+        rows[pl.ds(n, w, stride=w), :] = own_ref[:, n * w : (n + 1) * w].astype(jnp.float32)
     for a in range(w):
         part = slice(a * w, (a + 1) * w)
-        ladder = own_rows[part, :] - turned[:, part]
-        shift = shift_bc + shift_a_ref[a]
-        sum_ref[a] = 2.0 * ladder + shift * amps_ref[a].astype(jnp.float32)
-
-
-def finish(ab_ref, sum_ref, out_ref):
-    w = ab_ref.shape[0]
-    twice = 2.0 * ab_ref[...].astype(jnp.float32)
-    for a in range(w):
-        out_ref[a] = (sum_ref[a] - twice[:, a * w : (a + 1) * w]).astype(jnp.bfloat16)
+        ladder = rows[part, :] - ab_ref[:, part].astype(jnp.float32)
+        out_ref[a] = (sum_ref[a] + 2.0 * ladder).astype(jnp.bfloat16)
 
 
 def on_device(amplitudes, factors, energies):
@@ -193,20 +192,21 @@
     partial = pl.pallas_call(
         begin,
         out_shape=jax.ShapeDtypeStruct(amplitudes.shape, jnp.float32),
-        in_specs=[vmem, vmem, vmem, smem, vmem],
-        out_specs=vmem,
-        scratch_shapes=[pltpu.VMEM((w * w, w), jnp.float32)] * 2,
+        in_specs=[vmem, vmem, smem, vmem],
+        out_specs=vmem,
+        scratch_shapes=[pltpu.VMEM((w * w, w), jnp.float32)],
         compiler_params=params,
         name="begin",
-    )(own, swap_bc, amplitudes, energy_a, shift_bc)
+    )(swap_bc, amplitudes, energy_a, shift_bc)
     return pl.pallas_call(
         finish,
         out_shape=jax.ShapeDtypeStruct(amplitudes.shape, jnp.bfloat16),
-        in_specs=[vmem, vmem],
-        out_specs=vmem,
+        in_specs=[vmem, vmem, vmem],
+        out_specs=vmem,
+        scratch_shapes=[pltpu.VMEM((w * w, w), jnp.float32)],
         compiler_params=params,
         name="finish",
-    )(swap_ab, partial)
+    )(own, swap_ab, partial)
 
 
 def solution(mesh):

time: 97 us -> 96.5 us (level)
  the two profiles are of different devices: /device:TPU:129 before, /device:TPU:178 now
where the time goes in v5:
time: 96.5 us; the launch traced here: 96 us
  starting transfers between devices  46.9 us (49%)
  waiting for transfers between devices  37.2 us (39%)
  Pallas kernels  9.31 us (10%)
  local copies, waits for them, and re-layouts  2.31 us (2%)
    ppermute x3, starting transfers between devices, moved(): return lax.ppermute(array, ALL, pairs)  22.8 us
    ppermute x3, waiting for transfers between devices, moved(): return lax.ppermute(array, ALL, pairs)  20.4 us
    ppermute x1, starting transfers between devices, on_device(): far = lax.ppermute(near, 'zh', [(0, 1), (1, 0)])  10 us
    all_to_all x1, starting transfers between devices, on_device(): lax.all_to_all(parts, PLANE, split_axis=0, concat_axis=0, tiled=True)  7.4 us
    all_to_all x1, waiting for transfers between devices, on_device(): lax.all_to_all(parts, PLANE, split_axis=0, concat_axis=0, tiled=True)  6.88 us
    all_to_all x1, waiting for transfers between devices, on_device(): lax.all_to_all(close, PLANE, split_axis=0, concat_axis=0, tiled=True)[:24]  6.76 us
    all_to_all x1, starting transfers between devices, on_device(): lax.all_to_all(close, PLANE, split_axis=0, concat_axis=0, tiled=True)[:24]  6.76 us
    ppermute x1, waiting for transfers between devices, on_device(): far = lax.ppermute(near, 'zh', [(0, 1), (1, 0)])  3.21 us
  transfers between devices with their start and end apart: 6, of which 4 were waited for; matrix products, arithmetic and copies ran while one was open for 1% of the time, Pallas kernels for 4%

profile of v5, /device:TPU:178, one launch (start us, length us, event | category | flops | bytes accessed | tf_op | source)
XLA Modules:
  0.0 96.0 jit_solution(18392490527358880458)
XLA Ops:
  0.0 0.0 copy-start
  0.0 1.1 %copy-done = bf16[48,48,48]{2,1,0:T(8,128)(2,1)S(1)} copy-done((bf16[48,48,48]{2,1,0:T(8,128)(2,1)S(1)}, bf16[48,48,48]{2,1,0:T(8,128)(2,1)}, u32[]{:S(2)}) %copy-start) | copy-done | bytes 221208
  1.1 0.0 copy-start.2
  1.1 1.2 %pack.1 = bf16[32,48,96]{2,1,0:T(8,128)(2,1)} custom-call(bf16[48,48,48]{2,1,0:T(8,128)(2,1)S(1)} %copy-done), custom_call_target="tpu_custom_call" | custom-call | tf_op jit(solution)/shard_map/pack/pallas_call | solution.py:154
  2.2 7.4 %all-to-all-start = ((bf16[32,48,96]{2,1,0:T(8,128)(2,1)}), bf16[32,48,96]{2,1,0:T(8,128)(2,1)S(1)}, u32[]{:S(2)}, u32[]{:S(2)}) async-start(bf16[32,48,96]{2,1,0:T(8,128)(2,1)} %pack.1), calls=%async_computation | async-start | bytes 786432 | tf_op jit(solution)/shard_map/all_to_all | solution.py:163
  9.7 6.9 %all-to-all-done.rows_ref = bf16[32,48,96]{2,1,0:T(8,128)(2,1)S(1)} async-done(((bf16[32,48,96]{2,1,0:T(8,128)(2,1)}), bf16[32,48,96]{2,1,0:T(8,128)(2,1)S(1)}, u32[]{:S(2)}, u32[]{:S(2)}) %all-to-all-start) | async-done | bytes 294944 | tf_op jit(solution)/shard_map/all_to_all | solution.py:163
  16.6 0.1 concatenate.3
  16.7 10.0 %collective-permute-start = (bf16[48,960]{1,0:T(8,128)(2,1)S(1)}, bf16[48,960]{1,0:T(8,128)(2,1)S(1)}, u32[]{:S(2)}, u32[]{:S(2)}) collective-permute-start(bf16[48,960]{1,0:T(8,128)(2,1)S(1)} %concatenate.3), channel_id=1, source_target_pairs={{0,256},{256,0},{1,257},{257,1},{2,258},{258,2},{3,259},{259,3},{4... | collective-permute-start | bytes 276488 | tf_op jit(solution)/shard_map/ppermute | solution.py:166
  26.7 0.7 fusion.slot_ref
  27.4 0.0 copy-done.2
  27.4 2.3 %near_part.1 = (f32[2,192,384]{2,1,0:T(8,128)S(1)}, bf16[4,384,192]{2,1,0:T(8,128)(2,1)S(1)}) custom-call(s32[1]{0:T(128)} %bitcast.half_ref, bf16[32,48,96]{2,1,0:T(8,128)(2,1)S(1)} %all-to-all-done.rows_ref, bf16[4,384,384]{2,1,0:T(8,128)(2,1)S(1)} %copy-done.2), custom_call_target="tpu_custom_call" | custom-call | tf_op jit(solution)/shard_map/near_part/pallas_call | solution.py:167
  29.7 3.2 %collective-permute-done.far_ref = bf16[48,960]{1,0:T(8,128)(2,1)S(1)} collective-permute-done((bf16[48,960]{1,0:T(8,128)(2,1)S(1)}, bf16[48,960]{1,0:T(8,128)(2,1)S(1)}, u32[]{:S(2)}, u32[]{:S(2)}) %collective-permute-start) | collective-permute-done | bytes 92192 | tf_op jit(solution)/shard_map/ppermute | solution.py:166
  32.9 0.0 copy-start.3
  32.9 2.6 %far_part.1 = bf16[32,48,96]{2,1,0:T(8,128)(2,1)} custom-call(s32[1]{0:T(128)} %bitcast.half_ref, s32[32]{0:T(128)S(1)} %fusion.slot_ref, f32[2,192,384]{2,1,0:T(8,128)S(1)} %get-tuple-element.7.total_ref, bf16[48,960]{1,0:T(8,128)(2,1)S(1)} %collective-permute-done.far_ref, bf16[4,384,192]{2,1,0:T(8,128)(2,1)S(1)} %get-tuple-element.8.other_ref), custom_call_target="tpu_custom_call" | custom-call | tf_op jit(solution)/shard_map/far_part/pallas_call | solution.py:179
  35.5 0.0 copy-start.1
  35.5 6.8 %all-to-all-start.1 = ((bf16[32,48,96]{2,1,0:T(8,128)(2,1)}), bf16[32,48,96]{2,1,0:T(8,128)(2,1)S(1)}, u32[]{:S(2)}, u32[]{:S(2)}) async-start(bf16[32,48,96]{2,1,0:T(8,128)(2,1)} %far_part.1), calls=%async_computation.1 | async-start | bytes 786432 | tf_op jit(solution)/shard_map/all_to_all | solution.py:187
  42.3 0.0 copy-done.3
  42.3 0.1 fusion.1
  42.4 6.8 %all-to-all-done.1 = bf16[32,48,96]{2,1,0:T(8,128)(2,1)S(1)} async-done(((bf16[32,48,96]{2,1,0:T(8,128)(2,1)}), bf16[32,48,96]{2,1,0:T(8,128)(2,1)S(1)}, u32[]{:S(2)}, u32[]{:S(2)}) %all-to-all-start.1) | async-done | bytes 294944 | tf_op jit(solution)/shard_map/all_to_all | solution.py:187
  49.2 0.1 copy.5
  49.3 0.2 reshape.14
  49.5 7.9 %collective-permute-start.3 = (bf16[48,2304]{1,0:T(8,128)(2,1)S(1)}, bf16[48,2304]{1,0:T(8,128)(2,1)S(1)}, u32[]{:S(2)}, u32[]{:S(2)}) collective-permute-start(bf16[48,2304]{1,0:T(8,128)(2,1)S(1)} %reshape.14), channel_id=1, source_target_pairs={{0,0},{194,8},{64,16},{4,24},{5,32},{1,40},{68,48},{198,56},{12,1}... | collective-permute-start | bytes 663560 | tf_op jit(solution)/shard_map/ppermute | solution.py:47
  57.5 12.9 %collective-permute-start.2 = (bf16[48,2304]{1,0:T(8,128)(2,1)S(1)}, bf16[48,2304]{1,0:T(8,128)(2,1)S(1)}, u32[]{:S(2)}, u32[]{:S(2)}) collective-permute-start(bf16[48,2304]{1,0:T(8,128)(2,1)S(1)} %reshape.14), channel_id=1, source_target_pairs={{0,0},{194,1},{64,2},{4,3},{5,4},{1,5},{68,6},{198,7},{12,64},{206... | collective-permute-start | bytes 663560 | tf_op jit(solution)/shard_map/ppermute | solution.py:47
  70.4 1.9 %collective-permute-start.1 = (bf16[48,2304]{1,0:T(8,128)(2,1)S(1)}, bf16[48,2304]{1,0:T(8,128)(2,1)S(1)}, u32[]{:S(2)}, u32[]{:S(2)}) collective-permute-start(bf16[48,2304]{1,0:T(8,128)(2,1)S(1)} %reshape.14), channel_id=1, source_target_pairs={{0,0},{194,1},{64,2},{4,3},{5,4},{1,5},{68,6},{198,7},{12,8},{206,... | collective-permute-start | bytes 663560 | tf_op jit(solution)/shard_map/ppermute | solution.py:47
  72.3 0.1 broadcast_add_fusion.shift_bc_ref
  72.4 0.0 collective-permute-done.3.bc_ref
  72.4 0.0 copy-done.1
  72.4 1.6 %begin.1.sum_ref = f32[48,48,48]{2,1,0:T(8,128)S(1)} custom-call(bf16[48,2304]{1,0:T(8,128)(2,1)S(1)} %collective-permute-done.3.bc_ref, bf16[48,48,48]{2,1,0:T(8,128)(2,1)S(1)} %copy-done.1, f32[48]{0:T(128)S(1)} %get-tuple-element.20.shift_a_ref, f32[48,48]{1,0:T(8,128)S(1)} %broadcast_add_fusion.shift_bc_ref), custom_call_target="tpu_custom_call" | custom-call | tf_op jit(solution)/shard_map/begin/pallas_call | solution.py:192
  74.0 20.4 %collective-permute-done.2.ab_ref = bf16[48,2304]{1,0:T(8,128)(2,1)S(1)} collective-permute-done((bf16[48,2304]{1,0:T(8,128)(2,1)S(1)}, bf16[48,2304]{1,0:T(8,128)(2,1)S(1)}, u32[]{:S(2)}, u32[]{:S(2)}) %collective-permute-start.2) | collective-permute-done | bytes 221216 | tf_op jit(solution)/shard_map/ppermute | solution.py:47
  94.4 0.0 collective-permute-done.1.own_ref
  94.4 1.6 %finish.1 = bf16[48,48,48]{2,1,0:T(8,128)(2,1)} custom-call(bf16[48,2304]{1,0:T(8,128)(2,1)S(1)} %collective-permute-done.1.own_ref, bf16[48,2304]{1,0:T(8,128)(2,1)S(1)} %collective-permute-done.2.ab_ref, f32[48,48,48]{2,1,0:T(8,128)S(1)} %begin.1.sum_ref), custom_call_target="tpu_custom_call" | custom-call | tf_op jit(solution)/shard_map/finish/pallas_call | solution.py:201
  (2 shorter events, 0.0 us)
Async XLA Ops:
  0.0 1.1 %copy-start = (bf16[48,48,48]{2,1,0:T(8,128)(2,1)S(1)}, bf16[48,48,48]{2,1,0:T(8,128)(2,1)}, u32[]{:S(2)}) copy-start(bf16[48,48,48]{2,1,0:T(8,128)(2,1)} %amps_ref.3) | copy-start | bytes 663556
  1.1 26.3 %copy-start.2 = (bf16[4,384,384]{2,1,0:T(8,128)(2,1)S(1)}, bf16[4,384,384]{2,1,0:T(8,128)(2,1)}, u32[]{:S(2)}) copy-start(bf16[4,384,384]{2,1,0:T(8,128)(2,1)} %factors_ref.1) | copy-start | bytes 3538948
  2.2 14.3 %all-to-all-start = ((bf16[32,48,96]{2,1,0:T(8,128)(2,1)}), bf16[32,48,96]{2,1,0:T(8,128)(2,1)S(1)}, u32[]{:S(2)}, u32[]{:S(2)}) async-start(bf16[32,48,96]{2,1,0:T(8,128)(2,1)} %pack.1), calls=%async_computation | async-start | bytes 786432 | tf_op jit(solution)/shard_map/all_to_all | solution.py:163
  16.7 16.3 %collective-permute-start = (bf16[48,960]{1,0:T(8,128)(2,1)S(1)}, bf16[48,960]{1,0:T(8,128)(2,1)S(1)}, u32[]{:S(2)}, u32[]{:S(2)}) collective-permute-start(bf16[48,960]{1,0:T(8,128)(2,1)S(1)} %concatenate.3), channel_id=1, source_target_pairs={{0,256},{256,0},{1,257},{257,1},{2,258},{258,2},{3,259},{259,3},{4... | collective-permute-start | bytes 276488 | tf_op jit(solution)/shard_map/ppermute | solution.py:166
  32.9 9.4 %copy-start.3 = (f32[384]{0:T(512)S(1)}, f32[384]{0:T(512)}, u32[]{:S(2)}) copy-start(f32[384]{0:T(512)} %param.6) | copy-start | bytes 4612
  35.5 36.8 %copy-start.1 = (bf16[48,48,48]{2,1,0:T(8,128)(2,1)S(1)}, bf16[48,48,48]{2,1,0:T(8,128)(2,1)}, u32[]{:S(2)}) copy-start(bf16[48,48,48]{2,1,0:T(8,128)(2,1)} %amps_ref.3) | copy-start | bytes 663556
  35.5 13.6 %all-to-all-start.1 = ((bf16[32,48,96]{2,1,0:T(8,128)(2,1)}), bf16[32,48,96]{2,1,0:T(8,128)(2,1)S(1)}, u32[]{:S(2)}, u32[]{:S(2)}) async-start(bf16[32,48,96]{2,1,0:T(8,128)(2,1)} %far_part.1), calls=%async_computation.1 | async-start | bytes 786432 | tf_op jit(solution)/shard_map/all_to_all | solution.py:187
  49.5 22.9 %collective-permute-start.3 = (bf16[48,2304]{1,0:T(8,128)(2,1)S(1)}, bf16[48,2304]{1,0:T(8,128)(2,1)S(1)}, u32[]{:S(2)}, u32[]{:S(2)}) collective-permute-start(bf16[48,2304]{1,0:T(8,128)(2,1)S(1)} %reshape.14), channel_id=1, source_target_pairs={{0,0},{194,8},{64,16},{4,24},{5,32},{1,40},{68,48},{198,56},{12,1}... | collective-permute-start | bytes 663560 | tf_op jit(solution)/shard_map/ppermute | solution.py:47
  57.5 37.0 %collective-permute-start.2 = (bf16[48,2304]{1,0:T(8,128)(2,1)S(1)}, bf16[48,2304]{1,0:T(8,128)(2,1)S(1)}, u32[]{:S(2)}, u32[]{:S(2)}) collective-permute-start(bf16[48,2304]{1,0:T(8,128)(2,1)S(1)} %reshape.14), channel_id=1, source_target_pairs={{0,0},{194,1},{64,2},{4,3},{5,4},{1,5},{68,6},{198,7},{12,64},{206... | collective-permute-start | bytes 663560 | tf_op jit(solution)/shard_map/ppermute | solution.py:47
  70.4 24.0 %collective-permute-start.1 = (bf16[48,2304]{1,0:T(8,128)(2,1)S(1)}, bf16[48,2304]{1,0:T(8,128)(2,1)S(1)}, u32[]{:S(2)}, u32[]{:S(2)}) collective-permute-start(bf16[48,2304]{1,0:T(8,128)(2,1)S(1)} %reshape.14), channel_id=1, source_target_pairs={{0,0},{194,1},{64,2},{4,3},{5,4},{1,5},{68,6},{198,7},{12,8},{206,... | collective-permute-start | bytes 663560 | tf_op jit(solution)/shard_map/ppermute | solution.py:47

commit v6 on v5

--- a/solution.py
+++ b/solution.py
@@ -10,7 +10,7 @@
 
 ALL = ("zh", "y", "zl", "x", "core")
 PLANE = ("y", "x", "core")
-UPPER = [(u, v) for u in range(4) for v in range(u, 4)]
+UPPER = [(u, v) for u in range(4) for v in range(u + 1, 4)]
 LAST = (((1,), (1,)), ((), ()))
 PLACES = (
     (0, 26, 8, 4, 5, 1, 12, 30, 9, 10, 20, 2, 24, 22, 14, 6, 21, 15, 18, 28, 11, 16, 31, 23, 3, 27, 13, 17, 7, 29, 19, 25),
@@ -91,17 +91,20 @@
     w = far_ref.shape[0]
     own = pl.ds(pl.multiple_of(half_ref[0] * 4 * w, 64), 4 * w)
     mine = jnp.concatenate([other_ref[p, own, :] for p in range(4)], axis=0)
-    zero = jnp.zeros((w, w), jnp.bfloat16)
+    zero = jnp.zeros((w, w), jnp.float32)
+    row = lax.broadcasted_iota(jnp.int32, (w, w), 0)
+    column = lax.broadcasted_iota(jnp.int32, (w, w), 1)
     results = []
     for b in range(2):
-        blocks = {at: far_ref[:, (2 * n + b) * w : (2 * n + b + 1) * w] for n, at in enumerate(UPPER)}
-        upper = [[blocks[u, v] if u <= v else zero for v in range(4)] for u in range(4)]
-        strict = [[blocks[u, v] if u < v else zero for v in range(4)] for u in range(4)]
-        upper, strict = (
-            jnp.concatenate([jnp.concatenate(line, axis=1) for line in array], axis=0) for array in (upper, strict)
-        )
-        along = jnp.dot(mine, upper, preferred_element_type=jnp.float32)
-        along -= lax.dot_general(mine, strict, LAST, preferred_element_type=jnp.float32)
+        blocks = [far_ref[:, (2 * n + b) * w : (2 * n + b + 1) * w].astype(jnp.float32) for n in range(8)]
+        found = dict(zip(UPPER, blocks))
+        for n in range(2):
+            found[2 * n, 2 * n] = jnp.where(row < column, blocks[6 + n], zero)
+            found[2 * n + 1, 2 * n + 1] = jnp.where(row > column, blocks[6 + n], zero)
+        part = [jnp.concatenate([found.get((u, v), zero) for v in range(4)], axis=1) for u in range(4)]
+        part = jnp.concatenate(part, axis=0).astype(jnp.bfloat16)
+        along = jnp.dot(mine, part, preferred_element_type=jnp.float32)
+        along -= lax.dot_general(mine, part, LAST, preferred_element_type=jnp.float32)
         along = along.astype(jnp.bfloat16)
         total = total_ref[b]
         for p in range(4):
@@ -162,7 +165,9 @@
     )(amplitudes)
     parts = lax.all_to_all(parts, PLANE, split_axis=0, concat_axis=0, tiled=True)
     near = lax.dynamic_slice_in_dim(parts.reshape(4, 8, w, 2 * w), half * 4, 4, 1)
-    near = jnp.concatenate([near[u, v] for u, v in UPPER], axis=1)
+    above = np.arange(w)[:, None] < np.arange(2 * w)[None, :] % w
+    mixed = [jnp.where(above, near[2 * n, 2 * n], near[2 * n + 1, 2 * n + 1]) for n in range(2)]
+    near = jnp.concatenate([near[u, v] for u, v in UPPER] + mixed, axis=1)
     far = lax.ppermute(near, "zh", [(0, 1), (1, 0)])
     total, other = pl.pallas_call(
         near_part,

time: 96.5 us -> 94.4 us (0.978)
  starting transfers between devices: 46.9 us -> 45.3 us
    ppermute x3, starting transfers between devices: 22.8 us -> 21.2 us  [moved(): return lax.ppermute(array, ALL, pairs)]
where the time goes in v6:
time: 94.4 us; the launch traced here: 94 us
  starting transfers between devices  45.3 us (48%)
  waiting for transfers between devices  36.8 us (39%)
  Pallas kernels  9.36 us (10%)
  local copies, waits for them, and re-layouts  2.3 us (2%)
    ppermute x3, starting transfers between devices, moved(): return lax.ppermute(array, ALL, pairs)  21.2 us
    ppermute x3, waiting for transfers between devices, moved(): return lax.ppermute(array, ALL, pairs)  20.4 us
    ppermute x1, starting transfers between devices, on_device(): far = lax.ppermute(near, 'zh', [(0, 1), (1, 0)])  10 us
    all_to_all x1, starting transfers between devices, on_device(): lax.all_to_all(parts, PLANE, split_axis=0, concat_axis=0, tiled=True)  7.4 us
    all_to_all x1, waiting for transfers between devices, on_device(): lax.all_to_all(parts, PLANE, split_axis=0, concat_axis=0, tiled=True)  6.88 us
    all_to_all x1, waiting for transfers between devices, on_device(): lax.all_to_all(close, PLANE, split_axis=0, concat_axis=0, tiled=True)[:24]  6.76 us
    all_to_all x1, starting transfers between devices, on_device(): lax.all_to_all(close, PLANE, split_axis=0, concat_axis=0, tiled=True)[:24]  6.64 us
    ppermute x1, waiting for transfers between devices, on_device(): far = lax.ppermute(near, 'zh', [(0, 1), (1, 0)])  2.79 us
  transfers between devices with their start and end apart: 6, of which 4 were waited for; matrix products, arithmetic and copies ran while one was open for 1% of the time, Pallas kernels for 4%

profile of v6, /device:TPU:178, one launch (start us, length us, event | category | flops | bytes accessed | tf_op | source)
XLA Modules:
  0.0 94.0 jit_solution(7315335010089539204)
XLA Ops:
  0.0 0.0 copy-start.3
  0.0 0.0 copy-start
  0.0 1.1 %copy-done = bf16[48,48,48]{2,1,0:T(8,128)(2,1)S(1)} copy-done((bf16[48,48,48]{2,1,0:T(8,128)(2,1)S(1)}, bf16[48,48,48]{2,1,0:T(8,128)(2,1)}, u32[]{:S(2)}) %copy-start) | copy-done | bytes 221208
  1.1 0.0 copy-start.2
  1.1 1.2 %pack.1 = bf16[32,48,96]{2,1,0:T(8,128)(2,1)} custom-call(bf16[48,48,48]{2,1,0:T(8,128)(2,1)S(1)} %copy-done), custom_call_target="tpu_custom_call" | custom-call | tf_op jit(solution)/shard_map/pack/pallas_call | solution.py:157
  2.3 7.4 %all-to-all-start = ((bf16[32,48,96]{2,1,0:T(8,128)(2,1)}), bf16[32,48,96]{2,1,0:T(8,128)(2,1)S(1)}, u32[]{:S(2)}, u32[]{:S(2)}) async-start(bf16[32,48,96]{2,1,0:T(8,128)(2,1)} %pack.1), calls=%async_computation | async-start | bytes 786432 | tf_op jit(solution)/shard_map/all_to_all | solution.py:166
  9.7 6.9 %all-to-all-done.rows_ref = bf16[32,48,96]{2,1,0:T(8,128)(2,1)S(1)} async-done(((bf16[32,48,96]{2,1,0:T(8,128)(2,1)}), bf16[32,48,96]{2,1,0:T(8,128)(2,1)S(1)}, u32[]{:S(2)}, u32[]{:S(2)}) %all-to-all-start) | async-done | bytes 294944 | tf_op jit(solution)/shard_map/all_to_all | solution.py:166
  16.6 0.0 copy-done.3
  16.6 0.1 concatenate.3
  16.7 10.0 %collective-permute-start = (bf16[48,768]{1,0:T(8,128)(2,1)S(1)}, bf16[48,768]{1,0:T(8,128)(2,1)S(1)}, u32[]{:S(2)}, u32[]{:S(2)}) collective-permute-start(bf16[48,768]{1,0:T(8,128)(2,1)S(1)} %concatenate.3), channel_id=1, source_target_pairs={{0,256},{256,0},{1,257},{257,1},{2,258},{258,2},{3,259},{259,3},{4... | collective-permute-start | bytes 221192 | tf_op jit(solution)/shard_map/ppermute | solution.py:171
  26.7 0.7 fusion.2.slot_ref
  27.4 0.0 copy-done.2
  27.4 2.3 %near_part.1 = (f32[2,192,384]{2,1,0:T(8,128)S(1)}, bf16[4,384,192]{2,1,0:T(8,128)(2,1)S(1)}) custom-call(s32[1]{0:T(128)} %bitcast.half_ref, bf16[32,48,96]{2,1,0:T(8,128)(2,1)S(1)} %all-to-all-done.rows_ref, bf16[4,384,384]{2,1,0:T(8,128)(2,1)S(1)} %copy-done.2), custom_call_target="tpu_custom_call" | custom-call | tf_op jit(solution)/shard_map/near_part/pallas_call | solution.py:172
  29.7 2.8 %collective-permute-done.far_ref = bf16[48,768]{1,0:T(8,128)(2,1)S(1)} collective-permute-done((bf16[48,768]{1,0:T(8,128)(2,1)S(1)}, bf16[48,768]{1,0:T(8,128)(2,1)S(1)}, u32[]{:S(2)}, u32[]{:S(2)}) %collective-permute-start) | collective-permute-done | bytes 73760 | tf_op jit(solution)/shard_map/ppermute | solution.py:171
  32.5 0.0 copy-start.4
  32.5 2.6 %far_part.1 = bf16[32,48,96]{2,1,0:T(8,128)(2,1)} custom-call(s32[1]{0:T(128)} %bitcast.half_ref, s32[32]{0:T(128)S(1)} %fusion.2.slot_ref, f32[2,192,384]{2,1,0:T(8,128)S(1)} %get-tuple-element.7.total_ref, bf16[48,768]{1,0:T(8,128)(2,1)S(1)} %collective-permute-done.far_ref, bf16[4,384,192]{2,1,0:T(8,128)(2,1)S(1)} %get-tuple-element.8.other_ref), custom_call_target="tpu_custom_call" | custom-call | tf_op jit(solution)/shard_map/far_part/pallas_call | solution.py:184
  35.2 6.6 %all-to-all-start.1 = ((bf16[32,48,96]{2,1,0:T(8,128)(2,1)}), bf16[32,48,96]{2,1,0:T(8,128)(2,1)S(1)}, u32[]{:S(2)}, u32[]{:S(2)}) async-start(bf16[32,48,96]{2,1,0:T(8,128)(2,1)} %far_part.1), calls=%async_computation.1 | async-start | bytes 786432 | tf_op jit(solution)/shard_map/all_to_all | solution.py:192
  41.8 0.0 copy-done.4
  41.8 0.1 fusion.3
  41.9 6.8 %all-to-all-done.1 = bf16[32,48,96]{2,1,0:T(8,128)(2,1)S(1)} async-done(((bf16[32,48,96]{2,1,0:T(8,128)(2,1)}), bf16[32,48,96]{2,1,0:T(8,128)(2,1)S(1)}, u32[]{:S(2)}, u32[]{:S(2)}) %all-to-all-start.1) | async-done | bytes 294944 | tf_op jit(solution)/shard_map/all_to_all | solution.py:192
  48.7 0.1 copy.6
  48.8 0.2 reshape.14
  49.0 6.9 %collective-permute-start.3 = (bf16[48,2304]{1,0:T(8,128)(2,1)S(1)}, bf16[48,2304]{1,0:T(8,128)(2,1)S(1)}, u32[]{:S(2)}, u32[]{:S(2)}) collective-permute-start(bf16[48,2304]{1,0:T(8,128)(2,1)S(1)} %reshape.14), channel_id=1, source_target_pairs={{0,0},{194,8},{64,16},{4,24},{5,32},{1,40},{68,48},{198,56},{12,1}... | collective-permute-start | bytes 663560 | tf_op jit(solution)/shard_map/ppermute | solution.py:47
  55.9 12.4 %collective-permute-start.2 = (bf16[48,2304]{1,0:T(8,128)(2,1)S(1)}, bf16[48,2304]{1,0:T(8,128)(2,1)S(1)}, u32[]{:S(2)}, u32[]{:S(2)}) collective-permute-start(bf16[48,2304]{1,0:T(8,128)(2,1)S(1)} %reshape.14), channel_id=1, source_target_pairs={{0,0},{194,1},{64,2},{4,3},{5,4},{1,5},{68,6},{198,7},{12,64},{206... | collective-permute-start | bytes 663560 | tf_op jit(solution)/shard_map/ppermute | solution.py:47
  68.4 1.9 %collective-permute-start.1 = (bf16[48,2304]{1,0:T(8,128)(2,1)S(1)}, bf16[48,2304]{1,0:T(8,128)(2,1)S(1)}, u32[]{:S(2)}, u32[]{:S(2)}) collective-permute-start(bf16[48,2304]{1,0:T(8,128)(2,1)S(1)} %reshape.14), channel_id=1, source_target_pairs={{0,0},{194,1},{64,2},{4,3},{5,4},{1,5},{68,6},{198,7},{12,8},{206,... | collective-permute-start | bytes 663560 | tf_op jit(solution)/shard_map/ppermute | solution.py:47
  70.3 0.1 broadcast_add_fusion.shift_bc_ref
  70.4 0.0 collective-permute-done.3.bc_ref
  70.4 0.0 copy-done.1
  70.4 1.6 %begin.1.sum_ref = f32[48,48,48]{2,1,0:T(8,128)S(1)} custom-call(bf16[48,2304]{1,0:T(8,128)(2,1)S(1)} %collective-permute-done.3.bc_ref, bf16[48,48,48]{2,1,0:T(8,128)(2,1)S(1)} %copy-done.1, f32[48]{0:T(128)S(1)} %get-tuple-element.18.shift_a_ref, f32[48,48]{1,0:T(8,128)S(1)} %broadcast_add_fusion.shift_bc_ref), custom_call_target="tpu_custom_call" | custom-call | tf_op jit(solution)/shard_map/begin/pallas_call | solution.py:197
  72.0 20.3 %collective-permute-done.2.ab_ref = bf16[48,2304]{1,0:T(8,128)(2,1)S(1)} collective-permute-done((bf16[48,2304]{1,0:T(8,128)(2,1)S(1)}, bf16[48,2304]{1,0:T(8,128)(2,1)S(1)}, u32[]{:S(2)}, u32[]{:S(2)}) %collective-permute-start.2) | collective-permute-done | bytes 221216 | tf_op jit(solution)/shard_map/ppermute | solution.py:47
  92.4 0.0 collective-permute-done.1.own_ref
  92.4 1.6 %finish.1 = bf16[48,48,48]{2,1,0:T(8,128)(2,1)} custom-call(bf16[48,2304]{1,0:T(8,128)(2,1)S(1)} %collective-permute-done.1.own_ref, bf16[48,2304]{1,0:T(8,128)(2,1)S(1)} %collective-permute-done.2.ab_ref, f32[48,48,48]{2,1,0:T(8,128)S(1)} %begin.1.sum_ref), custom_call_target="tpu_custom_call" | custom-call | tf_op jit(solution)/shard_map/finish/pallas_call | solution.py:206
  (3 shorter events, 0.0 us)
Async XLA Ops:
  0.0 16.6 %copy-start.3 = (pred[1,1,48,96]{3,2,1,0:T(8,128)(4,1)S(1)}, pred[1,1,48,96]{3,2,1,0:T(8,128)(4,1)}, u32[]{:S(2)}) copy-start(pred[1,1,48,96]{3,2,1,0:T(8,128)(4,1)} %constant.40) | copy-start | bytes 13828
  0.0 1.1 %copy-start = (bf16[48,48,48]{2,1,0:T(8,128)(2,1)S(1)}, bf16[48,48,48]{2,1,0:T(8,128)(2,1)}, u32[]{:S(2)}) copy-start(bf16[48,48,48]{2,1,0:T(8,128)(2,1)} %amps_ref.3) | copy-start | bytes 663556
  1.1 26.3 %copy-start.2 = (bf16[4,384,384]{2,1,0:T(8,128)(2,1)S(1)}, bf16[4,384,384]{2,1,0:T(8,128)(2,1)}, u32[]{:S(2)}) copy-start(bf16[4,384,384]{2,1,0:T(8,128)(2,1)} %factors_ref.1) | copy-start | bytes 3538948
  2.3 14.3 %all-to-all-start = ((bf16[32,48,96]{2,1,0:T(8,128)(2,1)}), bf16[32,48,96]{2,1,0:T(8,128)(2,1)S(1)}, u32[]{:S(2)}, u32[]{:S(2)}) async-start(bf16[32,48,96]{2,1,0:T(8,128)(2,1)} %pack.1), calls=%async_computation | async-start | bytes 786432 | tf_op jit(solution)/shard_map/all_to_all | solution.py:166
  16.7 15.8 %collective-permute-start = (bf16[48,768]{1,0:T(8,128)(2,1)S(1)}, bf16[48,768]{1,0:T(8,128)(2,1)S(1)}, u32[]{:S(2)}, u32[]{:S(2)}) collective-permute-start(bf16[48,768]{1,0:T(8,128)(2,1)S(1)} %concatenate.3), channel_id=1, source_target_pairs={{0,256},{256,0},{1,257},{257,1},{2,258},{258,2},{3,259},{259,3},{4... | collective-permute-start | bytes 221192 | tf_op jit(solution)/shard_map/ppermute | solution.py:171
  32.5 9.3 %copy-start.4 = (f32[384]{0:T(512)S(1)}, f32[384]{0:T(512)}, u32[]{:S(2)}) copy-start(f32[384]{0:T(512)} %param.7) | copy-start | bytes 4612
  35.2 35.2 %copy-start.1 = (bf16[48,48,48]{2,1,0:T(8,128)(2,1)S(1)}, bf16[48,48,48]{2,1,0:T(8,128)(2,1)}, u32[]{:S(2)}) copy-start(bf16[48,48,48]{2,1,0:T(8,128)(2,1)} %amps_ref.3) | copy-start | bytes 663556
  35.2 13.5 %all-to-all-start.1 = ((bf16[32,48,96]{2,1,0:T(8,128)(2,1)}), bf16[32,48,96]{2,1,0:T(8,128)(2,1)S(1)}, u32[]{:S(2)}, u32[]{:S(2)}) async-start(bf16[32,48,96]{2,1,0:T(8,128)(2,1)} %far_part.1), calls=%async_computation.1 | async-start | bytes 786432 | tf_op jit(solution)/shard_map/all_to_all | solution.py:192
  49.0 21.3 %collective-permute-start.3 = (bf16[48,2304]{1,0:T(8,128)(2,1)S(1)}, bf16[48,2304]{1,0:T(8,128)(2,1)S(1)}, u32[]{:S(2)}, u32[]{:S(2)}) collective-permute-start(bf16[48,2304]{1,0:T(8,128)(2,1)S(1)} %reshape.14), channel_id=1, source_target_pairs={{0,0},{194,8},{64,16},{4,24},{5,32},{1,40},{68,48},{198,56},{12,1}... | collective-permute-start | bytes 663560 | tf_op jit(solution)/shard_map/ppermute | solution.py:47
  55.9 36.4 %collective-permute-start.2 = (bf16[48,2304]{1,0:T(8,128)(2,1)S(1)}, bf16[48,2304]{1,0:T(8,128)(2,1)S(1)}, u32[]{:S(2)}, u32[]{:S(2)}) collective-permute-start(bf16[48,2304]{1,0:T(8,128)(2,1)S(1)} %reshape.14), channel_id=1, source_target_pairs={{0,0},{194,1},{64,2},{4,3},{5,4},{1,5},{68,6},{198,7},{12,64},{206... | collective-permute-start | bytes 663560 | tf_op jit(solution)/shard_map/ppermute | solution.py:47
  68.4 24.0 %collective-permute-start.1 = (bf16[48,2304]{1,0:T(8,128)(2,1)S(1)}, bf16[48,2304]{1,0:T(8,128)(2,1)S(1)}, u32[]{:S(2)}, u32[]{:S(2)}) collective-permute-start(bf16[48,2304]{1,0:T(8,128)(2,1)S(1)} %reshape.14), channel_id=1, source_target_pairs={{0,0},{194,1},{64,2},{4,3},{5,4},{1,5},{68,6},{198,7},{12,8},{206,... | collective-permute-start | bytes 663560 | tf_op jit(solution)/shard_map/ppermute | solution.py:47

commit v7 on v6

--- a/solution.py
+++ b/solution.py
@@ -118,24 +118,25 @@
             out_ref[slot_ref[y * 8 + k]] = jnp.concatenate(tile, axis=1).astype(jnp.bfloat16)
 
 
-def begin(bc_ref, amps_ref, shift_a_ref, shift_bc_ref, sum_ref, rows):
+def begin(ab_ref, amps_ref, shift_a_ref, shift_bc_ref, sum_ref):
     w = amps_ref.shape[0]
     shift_bc = shift_bc_ref[...]
-    for n in range(w):
-        rows[pl.ds(n, w, stride=w), :] = bc_ref[:, n * w : (n + 1) * w].astype(jnp.float32)
-    turned = rows[...].T
     for a in range(w):
         shift = shift_bc + shift_a_ref[a]
-        sum_ref[a] = shift * amps_ref[a].astype(jnp.float32) - 2.0 * turned[:, a * w : (a + 1) * w]
-
-
-def finish(own_ref, ab_ref, sum_ref, out_ref, rows):
-    w = ab_ref.shape[0]
+        swapped = ab_ref[:, a * w : (a + 1) * w].astype(jnp.float32)
+        sum_ref[a] = shift * amps_ref[a].astype(jnp.float32) - 2.0 * swapped
+
+
+def finish(own_ref, bc_ref, sum_ref, out_ref, own_rows, bc_rows):
+    w = bc_ref.shape[0]
     for n in range(w):
-        rows[pl.ds(n, w, stride=w), :] = own_ref[:, n * w : (n + 1) * w].astype(jnp.float32)
+        part = slice(n * w, (n + 1) * w)
+        own_rows[pl.ds(n, w, stride=w), :] = own_ref[:, part].astype(jnp.float32)
+        bc_rows[pl.ds(n, w, stride=w), :] = bc_ref[:, part].astype(jnp.float32)
+    turned = bc_rows[...].T
     for a in range(w):
         part = slice(a * w, (a + 1) * w)
-        ladder = rows[part, :] - ab_ref[:, part].astype(jnp.float32)
+        ladder = own_rows[part, :] - turned[:, part]
         out_ref[a] = (sum_ref[a] + 2.0 * ladder).astype(jnp.bfloat16)
 
 
@@ -199,19 +200,18 @@
         out_shape=jax.ShapeDtypeStruct(amplitudes.shape, jnp.float32),
         in_specs=[vmem, vmem, smem, vmem],
         out_specs=vmem,
-        scratch_shapes=[pltpu.VMEM((w * w, w), jnp.float32)],
         compiler_params=params,
         name="begin",
-    )(swap_bc, amplitudes, energy_a, shift_bc)
+    )(swap_ab, amplitudes, energy_a, shift_bc)
     return pl.pallas_call(
         finish,
         out_shape=jax.ShapeDtypeStruct(amplitudes.shape, jnp.bfloat16),
         in_specs=[vmem, vmem, vmem],
         out_specs=vmem,
-        scratch_shapes=[pltpu.VMEM((w * w, w), jnp.float32)],
+        scratch_shapes=[pltpu.VMEM((w * w, w), jnp.float32)] * 2,
         compiler_params=params,
         name="finish",
-    )(own, swap_ab, partial)
+    )(own, swap_bc, partial)
 
 
 def solution(mesh):

time: 94.4 us -> 96.3 us (1.020)
  the two profiles are of different devices: /device:TPU:178 before, /device:TPU:31 now
where the time goes in v7:
time: 96.3 us; the launch traced here: 95.8 us
  starting transfers between devices  54.6 us (57%)
  waiting for transfers between devices  29.2 us (30%)
  Pallas kernels  9.49 us (10%)
  local copies, waits for them, and re-layouts  2.3 us (2%)
    ppermute x3, starting transfers between devices, moved(): return lax.ppermute(array, ALL, pairs)  23.3 us
    ppermute x3, waiting for transfers between devices, moved(): return lax.ppermute(array, ALL, pairs)  14.9 us
    ppermute x1, starting transfers between devices, on_device(): far = lax.ppermute(near, 'zh', [(0, 1), (1, 0)])  13.6 us
    all_to_all x1, starting transfers between devices, on_device(): lax.all_to_all(parts, PLANE, split_axis=0, concat_axis=0, tiled=True)  9.55 us
    all_to_all x1, starting transfers between devices, on_device(): lax.all_to_all(close, PLANE, split_axis=0, concat_axis=0, tiled=True)[:24]  8.12 us
    all_to_all x1, waiting for transfers between devices, on_device(): lax.all_to_all(parts, PLANE, split_axis=0, concat_axis=0, tiled=True)  7.19 us
    all_to_all x1, waiting for transfers between devices, on_device(): lax.all_to_all(close, PLANE, split_axis=0, concat_axis=0, tiled=True)[:24]  7.15 us
    pallas_call x1, Pallas kernels, on_device(): pl.pallas_call(far_part, out_shape=jax.ShapeDtypeStruct((32, w, 2 * w), j...  2.64 us
  transfers between devices with their start and end apart: 6, of which 3 were waited for; matrix products, arithmetic and copies ran while one was open for 1% of the time, Pallas kernels for 3%

profile of v7, /device:TPU:31, one launch (start us, length us, event | category | flops | bytes accessed | tf_op | source)
XLA Modules:
  0.0 95.8 jit_solution(14875843492207095682)
XLA Ops:
  0.0 0.0 copy-start.3
  0.0 0.0 copy-start
  0.0 1.1 %copy-done = bf16[48,48,48]{2,1,0:T(8,128)(2,1)S(1)} copy-done((bf16[48,48,48]{2,1,0:T(8,128)(2,1)S(1)}, bf16[48,48,48]{2,1,0:T(8,128)(2,1)}, u32[]{:S(2)}) %copy-start) | copy-done | bytes 221208
  1.1 0.0 copy-start.2
  1.1 1.2 %pack.1 = bf16[32,48,96]{2,1,0:T(8,128)(2,1)} custom-call(bf16[48,48,48]{2,1,0:T(8,128)(2,1)S(1)} %copy-done), custom_call_target="tpu_custom_call" | custom-call | tf_op jit(solution)/shard_map/pack/pallas_call | solution.py:158
  2.3 9.6 %all-to-all-start = ((bf16[32,48,96]{2,1,0:T(8,128)(2,1)}), bf16[32,48,96]{2,1,0:T(8,128)(2,1)S(1)}, u32[]{:S(2)}, u32[]{:S(2)}) async-start(bf16[32,48,96]{2,1,0:T(8,128)(2,1)} %pack.1), calls=%async_computation | async-start | bytes 786432 | tf_op jit(solution)/shard_map/all_to_all | solution.py:167
  11.8 7.2 %all-to-all-done.rows_ref = bf16[32,48,96]{2,1,0:T(8,128)(2,1)S(1)} async-done(((bf16[32,48,96]{2,1,0:T(8,128)(2,1)}), bf16[32,48,96]{2,1,0:T(8,128)(2,1)S(1)}, u32[]{:S(2)}, u32[]{:S(2)}) %all-to-all-start) | async-done | bytes 294944 | tf_op jit(solution)/shard_map/all_to_all | solution.py:167
  19.0 0.0 copy-done.3
  19.0 0.1 concatenate.3
  19.2 13.6 %collective-permute-start = (bf16[48,768]{1,0:T(8,128)(2,1)S(1)}, bf16[48,768]{1,0:T(8,128)(2,1)S(1)}, u32[]{:S(2)}, u32[]{:S(2)}) collective-permute-start(bf16[48,768]{1,0:T(8,128)(2,1)S(1)} %concatenate.3), channel_id=1, source_target_pairs={{0,256},{256,0},{1,257},{257,1},{2,258},{258,2},{3,259},{259,3},{4... | collective-permute-start | bytes 221192 | tf_op jit(solution)/shard_map/ppermute | solution.py:172
  32.7 0.7 fusion.2.slot_ref
  33.4 0.0 copy-done.2
  33.4 2.3 %near_part.1 = (f32[2,192,384]{2,1,0:T(8,128)S(1)}, bf16[4,384,192]{2,1,0:T(8,128)(2,1)S(1)}) custom-call(s32[1]{0:T(128)} %bitcast.half_ref, bf16[32,48,96]{2,1,0:T(8,128)(2,1)S(1)} %all-to-all-done.rows_ref, bf16[4,384,384]{2,1,0:T(8,128)(2,1)S(1)} %copy-done.2), custom_call_target="tpu_custom_call" | custom-call | tf_op jit(solution)/shard_map/near_part/pallas_call | solution.py:173
  35.7 0.0 collective-permute-done.far_ref
  35.8 0.0 copy-start.4
  35.8 2.6 %far_part.1 = bf16[32,48,96]{2,1,0:T(8,128)(2,1)} custom-call(s32[1]{0:T(128)} %bitcast.half_ref, s32[32]{0:T(128)S(1)} %fusion.2.slot_ref, f32[2,192,384]{2,1,0:T(8,128)S(1)} %get-tuple-element.7.total_ref, bf16[48,768]{1,0:T(8,128)(2,1)S(1)} %collective-permute-done.far_ref, bf16[4,384,192]{2,1,0:T(8,128)(2,1)S(1)} %get-tuple-element.8.other_ref), custom_call_target="tpu_custom_call" | custom-call | tf_op jit(solution)/shard_map/far_part/pallas_call | solution.py:185
  38.4 8.1 %all-to-all-start.1 = ((bf16[32,48,96]{2,1,0:T(8,128)(2,1)}), bf16[32,48,96]{2,1,0:T(8,128)(2,1)S(1)}, u32[]{:S(2)}, u32[]{:S(2)}) async-start(bf16[32,48,96]{2,1,0:T(8,128)(2,1)} %far_part.1), calls=%async_computation.1 | async-start | bytes 786432 | tf_op jit(solution)/shard_map/all_to_all | solution.py:193
  46.6 0.0 copy-done.4
  46.6 0.1 fusion.3
  46.6 7.1 %all-to-all-done.1 = bf16[32,48,96]{2,1,0:T(8,128)(2,1)S(1)} async-done(((bf16[32,48,96]{2,1,0:T(8,128)(2,1)}), bf16[32,48,96]{2,1,0:T(8,128)(2,1)S(1)}, u32[]{:S(2)}, u32[]{:S(2)}) %all-to-all-start.1) | async-done | bytes 294944 | tf_op jit(solution)/shard_map/all_to_all | solution.py:193
  53.8 0.1 copy.6
  53.9 0.2 reshape.14
  54.1 4.6 %collective-permute-start.3 = (bf16[48,2304]{1,0:T(8,128)(2,1)S(1)}, bf16[48,2304]{1,0:T(8,128)(2,1)S(1)}, u32[]{:S(2)}, u32[]{:S(2)}) collective-permute-start(bf16[48,2304]{1,0:T(8,128)(2,1)S(1)} %reshape.14), channel_id=1, source_target_pairs={{0,0},{194,1},{64,2},{4,3},{5,4},{1,5},{68,6},{198,7},{12,64},{206... | collective-permute-start | bytes 663560 | tf_op jit(solution)/shard_map/ppermute | solution.py:47
  58.8 15.3 %collective-permute-start.2 = (bf16[48,2304]{1,0:T(8,128)(2,1)S(1)}, bf16[48,2304]{1,0:T(8,128)(2,1)S(1)}, u32[]{:S(2)}, u32[]{:S(2)}) collective-permute-start(bf16[48,2304]{1,0:T(8,128)(2,1)S(1)} %reshape.14), channel_id=1, source_target_pairs={{0,0},{194,8},{64,16},{4,24},{5,32},{1,40},{68,48},{198,56},{12,1}... | collective-permute-start | bytes 663560 | tf_op jit(solution)/shard_map/ppermute | solution.py:47
  74.1 3.4 %collective-permute-start.1 = (bf16[48,2304]{1,0:T(8,128)(2,1)S(1)}, bf16[48,2304]{1,0:T(8,128)(2,1)S(1)}, u32[]{:S(2)}, u32[]{:S(2)}) collective-permute-start(bf16[48,2304]{1,0:T(8,128)(2,1)S(1)} %reshape.14), channel_id=1, source_target_pairs={{0,0},{194,1},{64,2},{4,3},{5,4},{1,5},{68,6},{198,7},{12,8},{206,... | collective-permute-start | bytes 663560 | tf_op jit(solution)/shard_map/ppermute | solution.py:47
  77.5 0.1 broadcast_add_fusion.shift_bc_ref
  77.6 0.0 collective-permute-done.3.ab_ref
  77.6 0.0 copy-done.1
  77.6 1.0 begin.1.sum_ref
  78.5 14.9 %collective-permute-done.2.bc_ref = bf16[48,2304]{1,0:T(8,128)(2,1)S(1)} collective-permute-done((bf16[48,2304]{1,0:T(8,128)(2,1)S(1)}, bf16[48,2304]{1,0:T(8,128)(2,1)S(1)}, u32[]{:S(2)}, u32[]{:S(2)}) %collective-permute-start.2) | collective-permute-done | bytes 221216 | tf_op jit(solution)/shard_map/ppermute | solution.py:47
  93.4 0.0 collective-permute-done.1.own_ref
  93.4 2.4 %finish.1 = bf16[48,48,48]{2,1,0:T(8,128)(2,1)} custom-call(bf16[48,2304]{1,0:T(8,128)(2,1)S(1)} %collective-permute-done.1.own_ref, bf16[48,2304]{1,0:T(8,128)(2,1)S(1)} %collective-permute-done.2.bc_ref, f32[48,48,48]{2,1,0:T(8,128)S(1)} %begin.1.sum_ref), custom_call_target="tpu_custom_call" | custom-call | tf_op jit(solution)/shard_map/finish/pallas_call | solution.py:206
  (3 shorter events, 0.0 us)
Async XLA Ops:
  0.0 19.0 %copy-start.3 = (pred[1,1,48,96]{3,2,1,0:T(8,128)(4,1)S(1)}, pred[1,1,48,96]{3,2,1,0:T(8,128)(4,1)}, u32[]{:S(2)}) copy-start(pred[1,1,48,96]{3,2,1,0:T(8,128)(4,1)} %constant.40) | copy-start | bytes 13828
  0.0 1.1 %copy-start = (bf16[48,48,48]{2,1,0:T(8,128)(2,1)S(1)}, bf16[48,48,48]{2,1,0:T(8,128)(2,1)}, u32[]{:S(2)}) copy-start(bf16[48,48,48]{2,1,0:T(8,128)(2,1)} %amps_ref.3) | copy-start | bytes 663556
  1.1 32.3 %copy-start.2 = (bf16[4,384,384]{2,1,0:T(8,128)(2,1)S(1)}, bf16[4,384,384]{2,1,0:T(8,128)(2,1)}, u32[]{:S(2)}) copy-start(bf16[4,384,384]{2,1,0:T(8,128)(2,1)} %factors_ref.1) | copy-start | bytes 3538948
  2.3 16.8 %all-to-all-start = ((bf16[32,48,96]{2,1,0:T(8,128)(2,1)}), bf16[32,48,96]{2,1,0:T(8,128)(2,1)S(1)}, u32[]{:S(2)}, u32[]{:S(2)}) async-start(bf16[32,48,96]{2,1,0:T(8,128)(2,1)} %pack.1), calls=%async_computation | async-start | bytes 786432 | tf_op jit(solution)/shard_map/all_to_all | solution.py:167
  19.2 16.6 %collective-permute-start = (bf16[48,768]{1,0:T(8,128)(2,1)S(1)}, bf16[48,768]{1,0:T(8,128)(2,1)S(1)}, u32[]{:S(2)}, u32[]{:S(2)}) collective-permute-start(bf16[48,768]{1,0:T(8,128)(2,1)S(1)} %concatenate.3), channel_id=1, source_target_pairs={{0,256},{256,0},{1,257},{257,1},{2,258},{258,2},{3,259},{259,3},{4... | collective-permute-start | bytes 221192 | tf_op jit(solution)/shard_map/ppermute | solution.py:172
  35.8 10.8 %copy-start.4 = (f32[384]{0:T(512)S(1)}, f32[384]{0:T(512)}, u32[]{:S(2)}) copy-start(f32[384]{0:T(512)} %param.7) | copy-start | bytes 4612
  38.4 39.2 %copy-start.1 = (bf16[48,48,48]{2,1,0:T(8,128)(2,1)S(1)}, bf16[48,48,48]{2,1,0:T(8,128)(2,1)}, u32[]{:S(2)}) copy-start(bf16[48,48,48]{2,1,0:T(8,128)(2,1)} %amps_ref.3) | copy-start | bytes 663556
  38.4 15.4 %all-to-all-start.1 = ((bf16[32,48,96]{2,1,0:T(8,128)(2,1)}), bf16[32,48,96]{2,1,0:T(8,128)(2,1)S(1)}, u32[]{:S(2)}, u32[]{:S(2)}) async-start(bf16[32,48,96]{2,1,0:T(8,128)(2,1)} %far_part.1), calls=%async_computation.1 | async-start | bytes 786432 | tf_op jit(solution)/shard_map/all_to_all | solution.py:193
  54.1 23.4 %collective-permute-start.3 = (bf16[48,2304]{1,0:T(8,128)(2,1)S(1)}, bf16[48,2304]{1,0:T(8,128)(2,1)S(1)}, u32[]{:S(2)}, u32[]{:S(2)}) collective-permute-start(bf16[48,2304]{1,0:T(8,128)(2,1)S(1)} %reshape.14), channel_id=1, source_target_pairs={{0,0},{194,1},{64,2},{4,3},{5,4},{1,5},{68,6},{198,7},{12,64},{206... | collective-permute-start | bytes 663560 | tf_op jit(solution)/shard_map/ppermute | solution.py:47
  58.8 34.6 %collective-permute-start.2 = (bf16[48,2304]{1,0:T(8,128)(2,1)S(1)}, bf16[48,2304]{1,0:T(8,128)(2,1)S(1)}, u32[]{:S(2)}, u32[]{:S(2)}) collective-permute-start(bf16[48,2304]{1,0:T(8,128)(2,1)S(1)} %reshape.14), channel_id=1, source_target_pairs={{0,0},{194,8},{64,16},{4,24},{5,32},{1,40},{68,48},{198,56},{12,1}... | collective-permute-start | bytes 663560 | tf_op jit(solution)/shard_map/ppermute | solution.py:47
  74.1 19.3 %collective-permute-start.1 = (bf16[48,2304]{1,0:T(8,128)(2,1)S(1)}, bf16[48,2304]{1,0:T(8,128)(2,1)S(1)}, u32[]{:S(2)}, u32[]{:S(2)}) collective-permute-start(bf16[48,2304]{1,0:T(8,128)(2,1)S(1)} %reshape.14), channel_id=1, source_target_pairs={{0,0},{194,1},{64,2},{4,3},{5,4},{1,5},{68,6},{198,7},{12,8},{206,... | collective-permute-start | bytes 663560 | tf_op jit(solution)/shard_map/ppermute | solution.py:47

commit v8 on v6

--- a/solution.py
+++ b/solution.py
@@ -13,22 +13,22 @@
 UPPER = [(u, v) for u in range(4) for v in range(u + 1, 4)]
 LAST = (((1,), (1,)), ((), ()))
 PLACES = (
-    (0, 26, 8, 4, 5, 1, 12, 30, 9, 10, 20, 2, 24, 22, 14, 6, 21, 15, 18, 28, 11, 16, 31, 23, 3, 27, 13, 17, 7, 29, 19, 25),
-    (4, 30, 2, 6, 0, 10, 31, 1, 12, 14, 15, 8, 11, 13, 16, 20, 18, 22, 28, 9, 29, 21, 24, 3, 25, 26, 19, 27, 17, 23, 5, 7),
-    (2, 24, 28, 0, 30, 6, 10, 12, 8, 31, 11, 20, 13, 4, 3, 14, 22, 16, 17, 18, 23, 19, 21, 25, 7, 1, 29, 15, 26, 27, 5, 9),
-    (6, 28, 30, 0, 12, 10, 2, 22, 20, 8, 14, 7, 11, 18, 4, 16, 26, 15, 21, 9, 13, 23, 24, 3, 5, 17, 1, 27, 31, 19, 25, 29),
-    (8, 2, 26, 3, 30, 4, 12, 0, 20, 14, 5, 9, 15, 6, 18, 16, 22, 24, 10, 25, 19, 13, 7, 21, 28, 11, 23, 17, 29, 1, 31, 27),
-    (16, 0, 4, 22, 18, 12, 24, 26, 10, 14, 15, 8, 2, 9, 11, 20, 28, 3, 1, 27, 19, 30, 23, 13, 17, 5, 6, 29, 31, 7, 25, 21),
-    (30, 12, 2, 24, 28, 14, 0, 4, 10, 16, 8, 29, 13, 6, 15, 26, 25, 11, 22, 20, 17, 21, 18, 23, 1, 27, 19, 3, 31, 7, 9, 5),
-    (8, 14, 20, 2, 24, 6, 4, 26, 16, 10, 18, 30, 5, 0, 12, 11, 17, 21, 15, 22, 9, 1, 13, 28, 3, 23, 29, 7, 25, 19, 31, 27),
-    (30, 12, 6, 2, 26, 4, 0, 18, 20, 3, 7, 8, 10, 1, 24, 13, 31, 25, 16, 27, 5, 22, 14, 21, 15, 28, 19, 17, 23, 9, 29, 11),
-    (12, 22, 28, 24, 30, 4, 8, 6, 2, 14, 10, 11, 13, 18, 7, 16, 19, 0, 20, 9, 15, 29, 25, 26, 23, 17, 21, 27, 3, 31, 5, 1),
-    (4, 12, 2, 6, 28, 18, 14, 8, 0, 3, 26, 5, 15, 7, 10, 19, 16, 22, 24, 20, 21, 27, 23, 25, 17, 30, 11, 13, 31, 29, 1, 9),
-    (24, 14, 28, 2, 8, 9, 20, 4, 15, 12, 0, 10, 21, 16, 13, 6, 22, 26, 3, 7, 11, 17, 18, 25, 5, 27, 1, 30, 23, 19, 29, 31),
-    (4, 0, 1, 12, 6, 5, 30, 2, 24, 26, 25, 22, 8, 14, 10, 20, 21, 18, 9, 16, 11, 28, 19, 15, 27, 17, 7, 29, 13, 3, 31, 23),
-    (4, 24, 18, 6, 2, 12, 0, 5, 13, 14, 10, 8, 3, 15, 9, 16, 17, 20, 22, 26, 11, 30, 1, 28, 21, 31, 25, 19, 27, 23, 29, 7),
-    (6, 26, 4, 28, 12, 7, 14, 0, 13, 8, 18, 9, 22, 10, 15, 2, 27, 29, 19, 16, 20, 24, 23, 21, 17, 30, 31, 1, 25, 3, 11, 5),
-    (30, 10, 31, 8, 16, 20, 2, 4, 14, 6, 28, 3, 9, 12, 11, 15, 22, 17, 7, 18, 0, 13, 1, 26, 27, 29, 19, 21, 5, 24, 23, 25),
+    (12, 26, 2, 8, 30, 3, 6, 0, 1, 10, 9, 22, 16, 14, 13, 20, 24, 23, 31, 27, 4, 18, 21, 17, 11, 7, 5, 28, 15, 19, 25, 29),
+    (14, 6, 26, 16, 24, 4, 30, 5, 12, 8, 20, 10, 22, 9, 11, 13, 27, 0, 2, 15, 21, 7, 18, 23, 1, 25, 28, 17, 19, 31, 3, 29),
+    (0, 4, 12, 26, 10, 8, 2, 14, 5, 20, 30, 13, 6, 27, 3, 9, 15, 24, 22, 18, 16, 19, 17, 23, 31, 28, 1, 29, 21, 7, 11, 25),
+    (2, 4, 10, 26, 16, 12, 3, 28, 14, 6, 18, 13, 0, 11, 15, 8, 9, 20, 17, 7, 22, 21, 23, 29, 1, 30, 19, 27, 31, 24, 5, 25),
+    (6, 12, 2, 26, 7, 3, 0, 8, 10, 20, 13, 16, 9, 21, 22, 14, 30, 11, 28, 18, 15, 4, 17, 24, 25, 1, 23, 29, 27, 5, 19, 31),
+    (24, 22, 0, 20, 4, 16, 5, 26, 12, 8, 14, 13, 10, 15, 9, 11, 28, 1, 2, 21, 23, 6, 27, 18, 25, 7, 29, 3, 17, 19, 30, 31),
+    (28, 14, 6, 8, 4, 5, 24, 26, 16, 30, 10, 2, 0, 12, 20, 3, 15, 25, 18, 9, 22, 21, 23, 11, 7, 13, 19, 31, 1, 17, 29, 27),
+    (0, 10, 12, 6, 2, 18, 4, 7, 11, 1, 26, 13, 14, 22, 3, 8, 19, 23, 15, 16, 17, 20, 21, 9, 28, 27, 24, 29, 30, 31, 5, 25),
+    (30, 2, 0, 4, 6, 3, 1, 26, 22, 8, 20, 9, 10, 14, 16, 12, 7, 24, 28, 17, 13, 29, 18, 23, 25, 11, 19, 27, 31, 21, 15, 5),
+    (4, 6, 26, 12, 14, 28, 22, 24, 10, 8, 20, 16, 11, 9, 13, 15, 23, 29, 17, 2, 0, 18, 7, 21, 30, 5, 27, 3, 25, 19, 1, 31),
+    (4, 2, 5, 18, 6, 28, 0, 26, 16, 14, 8, 12, 13, 10, 3, 7, 17, 22, 24, 19, 20, 15, 9, 23, 30, 29, 1, 31, 11, 21, 25, 27),
+    (6, 2, 0, 10, 26, 8, 20, 4, 12, 11, 18, 9, 22, 13, 14, 24, 5, 15, 30, 3, 7, 16, 17, 27, 1, 23, 28, 21, 29, 25, 19, 31),
+    (4, 0, 8, 5, 26, 30, 2, 6, 14, 22, 9, 1, 10, 20, 11, 7, 3, 12, 16, 23, 18, 31, 28, 21, 13, 15, 24, 27, 25, 17, 19, 29),
+    (30, 2, 4, 5, 0, 16, 6, 22, 14, 8, 3, 12, 10, 15, 11, 13, 7, 18, 28, 20, 17, 19, 24, 23, 9, 26, 27, 29, 25, 1, 21, 31),
+    (6, 26, 30, 18, 2, 4, 7, 14, 28, 5, 8, 3, 9, 12, 31, 10, 13, 19, 16, 20, 15, 22, 21, 24, 11, 0, 23, 25, 29, 17, 1, 27),
+    (28, 8, 2, 0, 14, 29, 6, 7, 10, 9, 22, 3, 4, 26, 15, 12, 24, 25, 11, 16, 17, 13, 18, 20, 27, 5, 21, 23, 19, 1, 30, 31),
 )
 
 

time: 94.4 us -> 96.2 us (1.019)
  the two profiles are of different devices: /device:TPU:178 before, /device:TPU:136 now
where the time goes in v8:
time: 96.2 us; the launch traced here: 95.8 us
  starting transfers between devices  42.9 us (45%)
  waiting for transfers between devices  40.9 us (43%)
  Pallas kernels  9.36 us (10%)
  local copies, waits for them, and re-layouts  2.3 us (2%)
    ppermute x3, starting transfers between devices, moved(): return lax.ppermute(array, ALL, pairs)  19.3 us
    ppermute x3, waiting for transfers between devices, moved(): return lax.ppermute(array, ALL, pairs)  19 us
    ppermute x1, starting transfers between devices, on_device(): far = lax.ppermute(near, 'zh', [(0, 1), (1, 0)])  10.9 us
    all_to_all x1, waiting for transfers between devices, on_device(): lax.all_to_all(parts, PLANE, split_axis=0, concat_axis=0, tiled=True)  8.55 us
    all_to_all x1, waiting for transfers between devices, on_device(): lax.all_to_all(close, PLANE, split_axis=0, concat_axis=0, tiled=True)[:24]  8.46 us
    all_to_all x1, starting transfers between devices, on_device(): lax.all_to_all(parts, PLANE, split_axis=0, concat_axis=0, tiled=True)  7.54 us
    all_to_all x1, starting transfers between devices, on_device(): lax.all_to_all(close, PLANE, split_axis=0, concat_axis=0, tiled=True)[:24]  5.18 us
    ppermute x1, waiting for transfers between devices, on_device(): far = lax.ppermute(near, 'zh', [(0, 1), (1, 0)])  4.97 us
  transfers between devices with their start and end apart: 6, of which 4 were waited for; matrix products, arithmetic and copies ran while one was open for 1% of the time, Pallas kernels for 4%

profile of v8, /device:TPU:136, one launch (start us, length us, event | category | flops | bytes accessed | tf_op | source)
XLA Modules:
  0.0 95.8 jit_solution(16901926399567003176)
XLA Ops:
  0.0 0.0 copy-start.3
  0.0 0.0 copy-start
  0.0 1.1 %copy-done = bf16[48,48,48]{2,1,0:T(8,128)(2,1)S(1)} copy-done((bf16[48,48,48]{2,1,0:T(8,128)(2,1)S(1)}, bf16[48,48,48]{2,1,0:T(8,128)(2,1)}, u32[]{:S(2)}) %copy-start) | copy-done | bytes 221208
  1.1 0.0 copy-start.2
  1.1 1.2 %pack.1 = bf16[32,48,96]{2,1,0:T(8,128)(2,1)} custom-call(bf16[48,48,48]{2,1,0:T(8,128)(2,1)S(1)} %copy-done), custom_call_target="tpu_custom_call" | custom-call | tf_op jit(solution)/shard_map/pack/pallas_call | solution.py:157
  2.3 7.5 %all-to-all-start = ((bf16[32,48,96]{2,1,0:T(8,128)(2,1)}), bf16[32,48,96]{2,1,0:T(8,128)(2,1)S(1)}, u32[]{:S(2)}, u32[]{:S(2)}) async-start(bf16[32,48,96]{2,1,0:T(8,128)(2,1)} %pack.1), calls=%async_computation | async-start | bytes 786432 | tf_op jit(solution)/shard_map/all_to_all | solution.py:166
  9.8 8.5 %all-to-all-done.rows_ref = bf16[32,48,96]{2,1,0:T(8,128)(2,1)S(1)} async-done(((bf16[32,48,96]{2,1,0:T(8,128)(2,1)}), bf16[32,48,96]{2,1,0:T(8,128)(2,1)S(1)}, u32[]{:S(2)}, u32[]{:S(2)}) %all-to-all-start) | async-done | bytes 294944 | tf_op jit(solution)/shard_map/all_to_all | solution.py:166
  18.4 0.0 copy-done.3
  18.4 0.1 concatenate.3
  18.5 10.9 %collective-permute-start = (bf16[48,768]{1,0:T(8,128)(2,1)S(1)}, bf16[48,768]{1,0:T(8,128)(2,1)S(1)}, u32[]{:S(2)}, u32[]{:S(2)}) collective-permute-start(bf16[48,768]{1,0:T(8,128)(2,1)S(1)} %concatenate.3), channel_id=1, source_target_pairs={{0,256},{256,0},{1,257},{257,1},{2,258},{258,2},{3,259},{259,3},{4... | collective-permute-start | bytes 221192 | tf_op jit(solution)/shard_map/ppermute | solution.py:171
  29.4 0.7 fusion.2.slot_ref
  30.1 0.0 copy-done.2
  30.1 2.3 %near_part.1 = (f32[2,192,384]{2,1,0:T(8,128)S(1)}, bf16[4,384,192]{2,1,0:T(8,128)(2,1)S(1)}) custom-call(s32[1]{0:T(128)} %bitcast.half_ref, bf16[32,48,96]{2,1,0:T(8,128)(2,1)S(1)} %all-to-all-done.rows_ref, bf16[4,384,384]{2,1,0:T(8,128)(2,1)S(1)} %copy-done.2), custom_call_target="tpu_custom_call" | custom-call | tf_op jit(solution)/shard_map/near_part/pallas_call | solution.py:172
  32.4 5.0 %collective-permute-done.far_ref = bf16[48,768]{1,0:T(8,128)(2,1)S(1)} collective-permute-done((bf16[48,768]{1,0:T(8,128)(2,1)S(1)}, bf16[48,768]{1,0:T(8,128)(2,1)S(1)}, u32[]{:S(2)}, u32[]{:S(2)}) %collective-permute-start) | collective-permute-done | bytes 73760 | tf_op jit(solution)/shard_map/ppermute | solution.py:171
  37.4 0.0 copy-start.4
  37.4 2.6 %far_part.1 = bf16[32,48,96]{2,1,0:T(8,128)(2,1)} custom-call(s32[1]{0:T(128)} %bitcast.half_ref, s32[32]{0:T(128)S(1)} %fusion.2.slot_ref, f32[2,192,384]{2,1,0:T(8,128)S(1)} %get-tuple-element.7.total_ref, bf16[48,768]{1,0:T(8,128)(2,1)S(1)} %collective-permute-done.far_ref, bf16[4,384,192]{2,1,0:T(8,128)(2,1)S(1)} %get-tuple-element.8.other_ref), custom_call_target="tpu_custom_call" | custom-call | tf_op jit(solution)/shard_map/far_part/pallas_call | solution.py:184
  40.0 5.2 %all-to-all-start.1 = ((bf16[32,48,96]{2,1,0:T(8,128)(2,1)}), bf16[32,48,96]{2,1,0:T(8,128)(2,1)S(1)}, u32[]{:S(2)}, u32[]{:S(2)}) async-start(bf16[32,48,96]{2,1,0:T(8,128)(2,1)} %far_part.1), calls=%async_computation.1 | async-start | bytes 786432 | tf_op jit(solution)/shard_map/all_to_all | solution.py:192
  45.3 0.0 copy-done.4
  45.3 0.1 fusion.3
  45.3 8.5 %all-to-all-done.1 = bf16[32,48,96]{2,1,0:T(8,128)(2,1)S(1)} async-done(((bf16[32,48,96]{2,1,0:T(8,128)(2,1)}), bf16[32,48,96]{2,1,0:T(8,128)(2,1)S(1)}, u32[]{:S(2)}, u32[]{:S(2)}) %all-to-all-start.1) | async-done | bytes 294944 | tf_op jit(solution)/shard_map/all_to_all | solution.py:192
  53.8 0.1 copy.6
  53.9 0.2 reshape.14
  54.1 5.3 %collective-permute-start.3 = (bf16[48,2304]{1,0:T(8,128)(2,1)S(1)}, bf16[48,2304]{1,0:T(8,128)(2,1)S(1)}, u32[]{:S(2)}, u32[]{:S(2)}) collective-permute-start(bf16[48,2304]{1,0:T(8,128)(2,1)S(1)} %reshape.14), channel_id=1, source_target_pairs={{68,0},{194,8},{2,16},{64,24},{198,32},{3,40},{6,48},{0,56},{78,1}... | collective-permute-start | bytes 663560 | tf_op jit(solution)/shard_map/ppermute | solution.py:47
  59.4 9.7 %collective-permute-start.2 = (bf16[48,2304]{1,0:T(8,128)(2,1)S(1)}, bf16[48,2304]{1,0:T(8,128)(2,1)S(1)}, u32[]{:S(2)}, u32[]{:S(2)}) collective-permute-start(bf16[48,2304]{1,0:T(8,128)(2,1)S(1)} %reshape.14), channel_id=1, source_target_pairs={{68,0},{194,1},{2,2},{64,3},{198,4},{3,5},{6,6},{0,7},{78,64},{14,... | collective-permute-start | bytes 663560 | tf_op jit(solution)/shard_map/ppermute | solution.py:47
  69.1 4.3 %collective-permute-start.1 = (bf16[48,2304]{1,0:T(8,128)(2,1)S(1)}, bf16[48,2304]{1,0:T(8,128)(2,1)S(1)}, u32[]{:S(2)}, u32[]{:S(2)}) collective-permute-start(bf16[48,2304]{1,0:T(8,128)(2,1)S(1)} %reshape.14), channel_id=1, source_target_pairs={{68,0},{194,1},{2,2},{64,3},{198,4},{3,5},{6,6},{0,7},{78,8},{14,9... | collective-permute-start | bytes 663560 | tf_op jit(solution)/shard_map/ppermute | solution.py:47
  73.5 0.1 broadcast_add_fusion.shift_bc_ref
  73.5 0.0 collective-permute-done.3.bc_ref
  73.5 0.0 copy-done.1
  73.5 1.6 %begin.1.sum_ref = f32[48,48,48]{2,1,0:T(8,128)S(1)} custom-call(bf16[48,2304]{1,0:T(8,128)(2,1)S(1)} %collective-permute-done.3.bc_ref, bf16[48,48,48]{2,1,0:T(8,128)(2,1)S(1)} %copy-done.1, f32[48]{0:T(128)S(1)} %get-tuple-element.18.shift_a_ref, f32[48,48]{1,0:T(8,128)S(1)} %broadcast_add_fusion.shift_bc_ref), custom_call_target="tpu_custom_call" | custom-call | tf_op jit(solution)/shard_map/begin/pallas_call | solution.py:197
  75.2 19.0 %collective-permute-done.2.ab_ref = bf16[48,2304]{1,0:T(8,128)(2,1)S(1)} collective-permute-done((bf16[48,2304]{1,0:T(8,128)(2,1)S(1)}, bf16[48,2304]{1,0:T(8,128)(2,1)S(1)}, u32[]{:S(2)}, u32[]{:S(2)}) %collective-permute-start.2) | collective-permute-done | bytes 221216 | tf_op jit(solution)/shard_map/ppermute | solution.py:47
  94.2 0.0 collective-permute-done.1.own_ref
  94.2 1.6 %finish.1 = bf16[48,48,48]{2,1,0:T(8,128)(2,1)} custom-call(bf16[48,2304]{1,0:T(8,128)(2,1)S(1)} %collective-permute-done.1.own_ref, bf16[48,2304]{1,0:T(8,128)(2,1)S(1)} %collective-permute-done.2.ab_ref, f32[48,48,48]{2,1,0:T(8,128)S(1)} %begin.1.sum_ref), custom_call_target="tpu_custom_call" | custom-call | tf_op jit(solution)/shard_map/finish/pallas_call | solution.py:206
  (3 shorter events, 0.0 us)
Async XLA Ops:
  0.0 18.4 %copy-start.3 = (pred[1,1,48,96]{3,2,1,0:T(8,128)(4,1)S(1)}, pred[1,1,48,96]{3,2,1,0:T(8,128)(4,1)}, u32[]{:S(2)}) copy-start(pred[1,1,48,96]{3,2,1,0:T(8,128)(4,1)} %constant.40) | copy-start | bytes 13828
  0.0 1.1 %copy-start = (bf16[48,48,48]{2,1,0:T(8,128)(2,1)S(1)}, bf16[48,48,48]{2,1,0:T(8,128)(2,1)}, u32[]{:S(2)}) copy-start(bf16[48,48,48]{2,1,0:T(8,128)(2,1)} %amps_ref.3) | copy-start | bytes 663556
  1.1 29.0 %copy-start.2 = (bf16[4,384,384]{2,1,0:T(8,128)(2,1)S(1)}, bf16[4,384,384]{2,1,0:T(8,128)(2,1)}, u32[]{:S(2)}) copy-start(bf16[4,384,384]{2,1,0:T(8,128)(2,1)} %factors_ref.1) | copy-start | bytes 3538948
  2.3 16.1 %all-to-all-start = ((bf16[32,48,96]{2,1,0:T(8,128)(2,1)}), bf16[32,48,96]{2,1,0:T(8,128)(2,1)S(1)}, u32[]{:S(2)}, u32[]{:S(2)}) async-start(bf16[32,48,96]{2,1,0:T(8,128)(2,1)} %pack.1), calls=%async_computation | async-start | bytes 786432 | tf_op jit(solution)/shard_map/all_to_all | solution.py:166
  18.5 18.9 %collective-permute-start = (bf16[48,768]{1,0:T(8,128)(2,1)S(1)}, bf16[48,768]{1,0:T(8,128)(2,1)S(1)}, u32[]{:S(2)}, u32[]{:S(2)}) collective-permute-start(bf16[48,768]{1,0:T(8,128)(2,1)S(1)} %concatenate.3), channel_id=1, source_target_pairs={{0,256},{256,0},{1,257},{257,1},{2,258},{258,2},{3,259},{259,3},{4... | collective-permute-start | bytes 221192 | tf_op jit(solution)/shard_map/ppermute | solution.py:171
  37.4 7.9 %copy-start.4 = (f32[384]{0:T(512)S(1)}, f32[384]{0:T(512)}, u32[]{:S(2)}) copy-start(f32[384]{0:T(512)} %param.7) | copy-start | bytes 4612
  40.0 33.5 %copy-start.1 = (bf16[48,48,48]{2,1,0:T(8,128)(2,1)S(1)}, bf16[48,48,48]{2,1,0:T(8,128)(2,1)}, u32[]{:S(2)}) copy-start(bf16[48,48,48]{2,1,0:T(8,128)(2,1)} %amps_ref.3) | copy-start | bytes 663556
  40.0 13.8 %all-to-all-start.1 = ((bf16[32,48,96]{2,1,0:T(8,128)(2,1)}), bf16[32,48,96]{2,1,0:T(8,128)(2,1)S(1)}, u32[]{:S(2)}, u32[]{:S(2)}) async-start(bf16[32,48,96]{2,1,0:T(8,128)(2,1)} %far_part.1), calls=%async_computation.1 | async-start | bytes 786432 | tf_op jit(solution)/shard_map/all_to_all | solution.py:192
  54.1 19.4 %collective-permute-start.3 = (bf16[48,2304]{1,0:T(8,128)(2,1)S(1)}, bf16[48,2304]{1,0:T(8,128)(2,1)S(1)}, u32[]{:S(2)}, u32[]{:S(2)}) collective-permute-start(bf16[48,2304]{1,0:T(8,128)(2,1)S(1)} %reshape.14), channel_id=1, source_target_pairs={{68,0},{194,8},{2,16},{64,24},{198,32},{3,40},{6,48},{0,56},{78,1}... | collective-permute-start | bytes 663560 | tf_op jit(solution)/shard_map/ppermute | solution.py:47
  59.4 34.8 %collective-permute-start.2 = (bf16[48,2304]{1,0:T(8,128)(2,1)S(1)}, bf16[48,2304]{1,0:T(8,128)(2,1)S(1)}, u32[]{:S(2)}, u32[]{:S(2)}) collective-permute-start(bf16[48,2304]{1,0:T(8,128)(2,1)S(1)} %reshape.14), channel_id=1, source_target_pairs={{68,0},{194,1},{2,2},{64,3},{198,4},{3,5},{6,6},{0,7},{78,64},{14,... | collective-permute-start | bytes 663560 | tf_op jit(solution)/shard_map/ppermute | solution.py:47
  69.1 25.0 %collective-permute-start.1 = (bf16[48,2304]{1,0:T(8,128)(2,1)S(1)}, bf16[48,2304]{1,0:T(8,128)(2,1)S(1)}, u32[]{:S(2)}, u32[]{:S(2)}) collective-permute-start(bf16[48,2304]{1,0:T(8,128)(2,1)S(1)} %reshape.14), channel_id=1, source_target_pairs={{68,0},{194,1},{2,2},{64,3},{198,4},{3,5},{6,6},{0,7},{78,8},{14,9... | collective-permute-start | bytes 663560 | tf_op jit(solution)/shard_map/ppermute | solution.py:47
